TPU v7x, 256 devices: a whole 4x4x8 slice. The times are simulated.
256 devices in a mesh: ctx: 32 (over z, y), ep: 8 (over x, core).
Axes of the slice: x: 4, y: 4, z: 8, core: 2. Of those that a mesh axis runs over, the one named last changes fastest.
Arguments:
- stream: bfloat16 [4096, 3072], P(('ctx', 'ep')), may hold values from -6 to 6
- query: bfloat16 [4096, 4096], P('ctx', 'ep'), may hold values from -2 to 2
- key: bfloat16 [4096, 4096], P('ctx', 'ep'), may hold values from -2 to 2
- value: bfloat16 [4096, 4096], P('ctx', 'ep'), may hold values from -6 to 6
- decay_rate: float32 [32], P('ep'), may hold values from 7.324219e-05 to 0.08
- out_weight: bfloat16 [4096, 3072], P('ep', 'ctx'), may hold values from -0.09375 to 0.09375
- norm_gain: float32 [3072], replicated, may hold values from 0.25 to 1.75
- router_weight: bfloat16 [3072, 16], replicated, may hold values from -0.109375 to 0.109375
- routes: int32 [4096, 2], P(('ctx', 'ep')), may hold values from 0 to 15, all different within a row; in each aligned block of 16 rows (0 to 15, 16 to 31, ...) at most 3 rows name the same one
- expert_gate: bfloat16 [3072, 73728], P(None, ('ep', 'ctx')), may hold values from -0.109375 to 0.109375
- expert_up: bfloat16 [3072, 73728], P(None, ('ep', 'ctx')), may hold values from -0.109375 to 0.109375
- expert_down: bfloat16 [73728, 3072], P(('ep', 'ctx')), may hold values from -0.09375 to 0.09375
Outputs:
- block_out: bfloat16 [4096, 3072], P(('ctx', 'ep'))
Inputs may be any that keep to these rules, and one draw needn't show every extreme that they name: `routes`: in each aligned block of 16 tokens (the tokens of one device) no expert is named more than 3 times, a bound that some block reaches.
All inputs are finite; a program needn't handle non-finite values.
Results may differ from a plain program's by a relative error of at most 0.017.
Values may be sent and summed in bfloat16 or wider, within the bound.
A program may use at most 128 MiB of HBM per device.

v0:
```python
import jax
import jax.numpy as jnp
from jax import lax
from jax.sharding import PartitionSpec as P

PRECISE = lax.Precision.HIGHEST
EPSILON = 1e-06


def shifted(shard, axis, by):
    devices = lax.axis_size(axis)
    pairs = [(i, i + by) for i in range(devices) if 0 <= i + by < devices]
    return lax.ppermute(shard, axis, pairs)


def body(
    stream,
    query,
    key,
    value,
    decay_rate,
    out_weight,
    norm_gain,
    router_weight,
    routes,
    expert_gate,
    expert_up,
    expert_down,
):
    length = query.shape[0]
    head_count = decay_rate.shape[0]
    ctx_count = lax.axis_size("ctx")
    ep_count = lax.axis_size("ep")
    query_heads = query.reshape(length, head_count, -1)
    key_heads = key.reshape(length, head_count, -1)
    value_heads = value.reshape(length, head_count, -1)
    positions = jnp.arange(length, dtype=jnp.float32)
    distance = positions[:, None] - positions[None, :]
    causal = distance >= 0
    decay_mask = jnp.where(
        causal[None],
        jnp.exp(-decay_rate[:, None, None] * jnp.where(causal, distance, 0.0)[None]),
        0.0,
    )
    scores = jnp.einsum("ihd,jhd->hij", query_heads, key_heads, preferred_element_type=jnp.float32)
    weights = (scores * decay_mask).astype(jnp.bfloat16)
    intra_part = jnp.einsum(
        "hij,jhd->ihd", weights, value_heads, preferred_element_type=jnp.float32
    )
    key_fade = jnp.exp(-decay_rate[None, :] * (length - 1.0 - positions[:, None]))
    local_state = jnp.einsum(
        "jhd,jhe->hde",
        key_heads.astype(jnp.float32) * key_fade[:, :, None],
        value_heads.astype(jnp.float32),
        precision=PRECISE,
    )
    fade_all = jnp.exp(-decay_rate * length)

    def advance(section_index, carry_state):
        return shifted(fade_all[:, None, None] * carry_state + local_state, "ctx", 1)

    incoming = lax.fori_loop(0, ctx_count - 1, advance, jnp.zeros_like(local_state))
    query_fade = jnp.exp(-decay_rate[None, :] * (positions[:, None] + 1.0))
    inter_part = jnp.einsum(
        "ihd,hde->ihe",
        query_heads.astype(jnp.float32) * query_fade[:, :, None],
        incoming,
        precision=PRECISE,
    )
    mixed = intra_part + inter_part
    normed = mixed * lax.rsqrt(jnp.mean(mixed * mixed, axis=-1, keepdims=True) + EPSILON)
    heads_out = normed.reshape(length, -1).astype(jnp.bfloat16)
    partial_value = jnp.dot(
        heads_out,
        lax.all_gather(out_weight, "ctx", axis=1, tiled=True),
        preferred_element_type=jnp.float32,
    )
    attended = lax.psum_scatter(
        partial_value.astype(jnp.bfloat16), "ep", scatter_dimension=0, tiled=True
    ).astype(jnp.float32)
    hidden = stream.astype(jnp.float32) + attended
    token_rows = (
        hidden * lax.rsqrt(jnp.mean(hidden * hidden, axis=-1, keepdims=True) + EPSILON) * norm_gain
    ).astype(jnp.bfloat16)
    logits = jnp.dot(token_rows, router_weight, preferred_element_type=jnp.float32)
    chosen = jnp.take_along_axis(logits, routes, axis=1)
    lifted = jax.nn.sigmoid(chosen)
    gate_share = lifted / jnp.sum(lifted, axis=1, keepdims=True)
    tok_count = routes.shape[0]
    row_width = token_rows.shape[1]
    experts = router_weight.shape[1]
    per_group = experts // ep_count
    capacity = max(2, 3 * tok_count // experts)
    slices = ctx_count // per_group
    route_flat = routes.reshape(-1)
    onehot = (route_flat[:, None] == jnp.arange(experts, dtype=jnp.int32)[None, :]).astype(
        jnp.int32
    )
    before = jnp.cumsum(onehot, axis=0) - onehot
    route_rank = jnp.sum(before * onehot, axis=1)
    slot_index = route_flat * capacity + route_rank
    placing = (
        slot_index[None, :] == jnp.arange(experts * capacity, dtype=jnp.int32)[:, None]
    ).astype(jnp.bfloat16)
    doubled = jnp.repeat(token_rows, 2, axis=0)
    outgoing = jnp.dot(placing, doubled, preferred_element_type=jnp.float32).astype(jnp.bfloat16)
    outgoing = outgoing.reshape(ep_count, per_group * capacity, row_width)
    arrived = lax.all_to_all(outgoing, "ep", split_axis=0, concat_axis=0, tiled=True)
    by_expert = arrived.reshape(ep_count, per_group, capacity, row_width).transpose(1, 0, 2, 3)
    fanned = jnp.repeat(by_expert, slices, axis=0)
    gathered = lax.all_to_all(fanned, "ctx", split_axis=0, concat_axis=0, tiled=True)
    flat_rows = gathered.reshape(-1, row_width)
    gate_part = jnp.dot(flat_rows, expert_gate, preferred_element_type=jnp.float32)
    up_part = jnp.dot(flat_rows, expert_up, preferred_element_type=jnp.float32)
    inner_act = (jax.nn.silu(gate_part) * up_part).astype(jnp.bfloat16)
    partial_out = jnp.dot(inner_act, expert_down, preferred_element_type=jnp.float32)
    partial_out = partial_out.reshape(ctx_count, ep_count, capacity, row_width)
    returned = lax.all_to_all(
        partial_out.astype(jnp.bfloat16), "ctx", split_axis=0, concat_axis=0, tiled=True
    ).astype(partial_out.dtype)
    summed = (
        returned.reshape(per_group, slices, ep_count, capacity, row_width)
        .sum(axis=1)
        .astype(jnp.bfloat16)
    )
    back_home = lax.all_to_all(
        summed.transpose(1, 0, 2, 3), "ep", split_axis=0, concat_axis=0, tiled=True
    )
    results = back_home.reshape(experts * capacity, row_width)
    routed = jnp.dot(placing.T, results, preferred_element_type=jnp.float32).reshape(
        tok_count, 2, row_width
    )
    mixed_out = jnp.sum(gate_share[:, :, None] * routed, axis=1)
    return (hidden + mixed_out).astype(jnp.bfloat16)


def solution(mesh):
    placed = (
        P(("ctx", "ep"), None),
        P("ctx", "ep"),
        P("ctx", "ep"),
        P("ctx", "ep"),
        P("ep"),
        P("ep", "ctx"),
        P(),
        P(),
        P(("ctx", "ep"), None),
        P(None, ("ep", "ctx")),
        P(None, ("ep", "ctx")),
        P(("ep", "ctx"), None),
    )
    return jax.shard_map(
        body, mesh=mesh, in_specs=placed, out_specs=P(("ctx", "ep"), None), check_vma=False
    )
```

profile of v0, /device:TPU:1, one launch (start us, length us, event | category | flops | bytes accessed | tf_op | source)
XLA Modules:
  0.0 758.5 jit_solution(463737103467720842)
XLA Ops:
  11.7 314.6 %while.10 = (s32[]{:T(128)}, f32[4,128,128]{2,1,0:T(8,128)S(1)}, f32[4]{0:T(128)S(1)}, f32[4,128,128]{2,1,0:T(8,128)S(1)}, s32[]{:T(128)}) while((s32[]{:T(128)}, f32[4,128,128]{2,1,0:T(8,128)S(1)}, f32[4]{0:T(128)S(1)}, f32[4,128,128]{2,1,0:T(8,128)S(1)}, s32[]{:T(128)}) %tuple.23), condition=%wide.region_1.2_spmd, body=%wide.region_0.1_spmd.sunk | while | flops 131074 | bytes 1835125 | solution.py:62
  61.1 7.2 collective-permute-start
  68.3 9.0 %collective-permute-done = f32[4,128,128]{2,1,0:T(8,128)S(1)} collective-permute-done((f32[4,128,128]{2,1,0:T(8,128)S(1)}, f32[4,128,128]{2,1,0:T(8,128)S(1)}, u32[]{:S(2)}, u32[]{:S(2)}) %collective-permute-start) | collective-permute-done | bytes 262176 | tf_op jit(solution)/shard_map/while/body/eval_jaxpr/ppermute | solution.py:13
  77.4 8.2 %collective-permute-start = (f32[4,128,128]{2,1,0:T(8,128)S(1)}, f32[4,128,128]{2,1,0:T(8,128)S(1)}, u32[]{:S(2)}, u32[]{:S(2)}) collective-permute-start(f32[4,128,128]{2,1,0:T(8,128)S(1)} %multiply_add_fusion.4), channel_id=1, source_target_pairs={{0,8},{8,16},{16,24},{24,32},{32,40},{40,48},{48,56},{56,64},{64,7... | collective-permute-start | bytes 786440 | tf_op jit(solution)/shard_map/while/body/eval_jaxpr/ppermute | solution.py:13
  99.6 6.8 collective-permute-start
  110.6 6.4 collective-permute-start
  122.1 6.8 collective-permute-start
  135.0 6.3 collective-permute-start
  183.7 6.4 collective-permute-start
  212.8 6.3 collective-permute-start
  224.3 6.8 collective-permute-start
  285.8 6.4 collective-permute-start
  314.9 6.3 collective-permute-start
  331.5 105.9 %reduce-scatter.2.cloned.1.call-done = bf16[16,3072]{1,0:T(8,128)(2,1)} async-done(((bf16[128,3072]{1,0:T(8,128)(2,1)}), bf16[16,3072]{1,0:T(8,128)(2,1)}) %reduce-scatter.2.cloned.1.call-update) | async-done | bytes 98320 | tf_op jit(solution)/shard_map/reduce_scatter | solution.py:78
  440.0 13.5 %all_to_all.20 = bf16[8,6,3072]{2,1,0:T(8,128)(2,1)S(1)} all-to-all(bf16[8,6,3072]{2,1,0:T(8,128)(2,1)S(1)} %reshape.204), channel_id=1, replica_groups=mesh['ctx'=32,'ep'=8] {'ep'}, dimensions={0} | all-to-all | bytes 589824 | tf_op jit(solution)/shard_map/all_to_all | solution.py:108
  454.3 114.7 %all_to_all.21 = bf16[32,8,3,3072]{3,1,2,0:T(8,128)(2,1)S(1)} all-to-all(bf16[32,8,3,3072]{3,1,2,0:T(8,128)(2,1)S(1)} %bitcast.67), channel_id=1, replica_groups=mesh['ctx'=32,'ep'=8] {'ctx'}, dimensions={0} | all-to-all | bytes 9437184 | tf_op jit(solution)/shard_map/all_to_all | solution.py:111
  569.0 7.1 copy.85
  576.1 12.3 %reshape.207 = bf16[768,3072]{1,0:T(8,128)(2,1)} reshape(bf16[32,8,3,3072]{3,2,1,0:T(4,128)(2,1)} %copy.85) | data formatting | bytes 9437184 | tf_op jit(solution)/shard_map/reshape | solution.py:112
  593.9 10.4 %convolution_convert_fusion = bf16[768,3072]{1,0:T(8,128)(2,1)} fusion(bf16[288,3072]{1,0:T(8,128)(2,1)S(1)} %copy-done, bf16[768,3072]{1,0:T(8,128)(2,1)} %reshape.207, bf16[3072,288]{0,1:T(8,128)(2,1)} %param.24, f32[768,288]{0,1:T(8,128)} %fusion.40), kind=kOutput, calls=%fused_computation.2 | convolution fusion | flops 2721595392 | bytes 13860864 | tf_op jit(solution)/shard_map/dot_general | solution.py:116
  604.2 11.7 %convert_element_type.68 = bf16[32,8,3,3072]{3,2,1,0:T(4,128)(2,1)} reshape(bf16[768,3072]{1,0:T(8,128)(2,1)} %convolution_convert_fusion) | data formatting | bytes 9437184 | tf_op jit(solution)/shard_map/convert_element_type | solution.py:119
  615.9 7.2 copy.86
  630.7 101.9 %all-to-all-done.2 = bf16[32,8,3,3072]{3,1,2,0:T(8,128)(2,1)} async-done(((bf16[32,8,3,3072]{3,1,2,0:T(8,128)(2,1)}), bf16[32,8,3,3072]{3,1,2,0:T(8,128)(2,1)}, u32[]{:S(2)}, u32[]{:S(2)}) %all-to-all-start.2) | async-done | bytes 4718624 | tf_op jit(solution)/shard_map/all_to_all | solution.py:118
  737.0 6.4 all-to-all-start.3
  743.5 6.8 all-to-all-done.3
  (149 shorter events, 263.4 us)
Async XLA Ops:
  6.5 320.5 %all-gather.2.cloned.1.call-start = ((), (), s32[]{:S(2)}) async-start(), calls=%async_computation.5 | async-start | bytes 3244032 | tf_op jit(solution)/shard_map/all_gather | solution.py:75
  7.3 430.2 %reduce-scatter.2.cloned.1.call-start = ((), (), s32[]{:S(2)}) async-start(), calls=%async_computation.6 | async-start | bytes 884736 | tf_op jit(solution)/shard_map/reduce_scatter | solution.py:78
  61.1 16.2 %collective-permute-start = (f32[4,128,128]{2,1,0:T(8,128)S(1)}, f32[4,128,128]{2,1,0:T(8,128)S(1)}, u32[]{:S(2)}, u32[]{:S(2)}) collective-permute-start(f32[4,128,128]{2,1,0:T(8,128)S(1)} %multiply_add_fusion.4), channel_id=1, source_target_pairs={{0,8},{8,16},{16,24},{24,32},{32,40},{40,48},{48,56},{56,64},{64,7... | collective-permute-start | bytes 786440 | tf_op jit(solution)/shard_map/while/body/eval_jaxpr/ppermute | solution.py:13
  77.4 12.2 %collective-permute-start = (f32[4,128,128]{2,1,0:T(8,128)S(1)}, f32[4,128,128]{2,1,0:T(8,128)S(1)}, u32[]{:S(2)}, u32[]{:S(2)}) collective-permute-start(f32[4,128,128]{2,1,0:T(8,128)S(1)} %multiply_add_fusion.4), channel_id=1, source_target_pairs={{0,8},{8,16},{16,24},{24,32},{32,40},{40,48},{48,56},{56,64},{64,7... | collective-permute-start | bytes 786440 | tf_op jit(solution)/shard_map/while/body/eval_jaxpr/ppermute | solution.py:13
  89.6 9.8 %collective-permute-start = (f32[4,128,128]{2,1,0:T(8,128)S(1)}, f32[4,128,128]{2,1,0:T(8,128)S(1)}, u32[]{:S(2)}, u32[]{:S(2)}) collective-permute-start(f32[4,128,128]{2,1,0:T(8,128)S(1)} %multiply_add_fusion.4), channel_id=1, source_target_pairs={{0,8},{8,16},{16,24},{24,32},{32,40},{40,48},{48,56},{56,64},{64,7... | collective-permute-start | bytes 786440 | tf_op jit(solution)/shard_map/while/body/eval_jaxpr/ppermute | solution.py:13
  99.6 10.9 %collective-permute-start = (f32[4,128,128]{2,1,0:T(8,128)S(1)}, f32[4,128,128]{2,1,0:T(8,128)S(1)}, u32[]{:S(2)}, u32[]{:S(2)}) collective-permute-start(f32[4,128,128]{2,1,0:T(8,128)S(1)} %multiply_add_fusion.4), channel_id=1, source_target_pairs={{0,8},{8,16},{16,24},{24,32},{32,40},{40,48},{48,56},{56,64},{64,7... | collective-permute-start | bytes 786440 | tf_op jit(solution)/shard_map/while/body/eval_jaxpr/ppermute | solution.py:13
  110.6 11.5 %collective-permute-start = (f32[4,128,128]{2,1,0:T(8,128)S(1)}, f32[4,128,128]{2,1,0:T(8,128)S(1)}, u32[]{:S(2)}, u32[]{:S(2)}) collective-permute-start(f32[4,128,128]{2,1,0:T(8,128)S(1)} %multiply_add_fusion.4), channel_id=1, source_target_pairs={{0,8},{8,16},{16,24},{24,32},{32,40},{40,48},{48,56},{56,64},{64,7... | collective-permute-start | bytes 786440 | tf_op jit(solution)/shard_map/while/body/eval_jaxpr/ppermute | solution.py:13
  122.1 12.7 %collective-permute-start = (f32[4,128,128]{2,1,0:T(8,128)S(1)}, f32[4,128,128]{2,1,0:T(8,128)S(1)}, u32[]{:S(2)}, u32[]{:S(2)}) collective-permute-start(f32[4,128,128]{2,1,0:T(8,128)S(1)} %multiply_add_fusion.4), channel_id=1, source_target_pairs={{0,8},{8,16},{16,24},{24,32},{32,40},{40,48},{48,56},{56,64},{64,7... | collective-permute-start | bytes 786440 | tf_op jit(solution)/shard_map/while/body/eval_jaxpr/ppermute | solution.py:13
  135.0 11.0 %collective-permute-start = (f32[4,128,128]{2,1,0:T(8,128)S(1)}, f32[4,128,128]{2,1,0:T(8,128)S(1)}, u32[]{:S(2)}, u32[]{:S(2)}) collective-permute-start(f32[4,128,128]{2,1,0:T(8,128)S(1)} %multiply_add_fusion.4), channel_id=1, source_target_pairs={{0,8},{8,16},{16,24},{24,32},{32,40},{40,48},{48,56},{56,64},{64,7... | collective-permute-start | bytes 786440 | tf_op jit(solution)/shard_map/while/body/eval_jaxpr/ppermute | solution.py:13
  164.5 9.5 %collective-permute-start = (f32[4,128,128]{2,1,0:T(8,128)S(1)}, f32[4,128,128]{2,1,0:T(8,128)S(1)}, u32[]{:S(2)}, u32[]{:S(2)}) collective-permute-start(f32[4,128,128]{2,1,0:T(8,128)S(1)} %multiply_add_fusion.4), channel_id=1, source_target_pairs={{0,8},{8,16},{16,24},{24,32},{32,40},{40,48},{48,56},{56,64},{64,7... | collective-permute-start | bytes 786440 | tf_op jit(solution)/shard_map/while/body/eval_jaxpr/ppermute | solution.py:13
  174.1 9.5 %collective-permute-start = (f32[4,128,128]{2,1,0:T(8,128)S(1)}, f32[4,128,128]{2,1,0:T(8,128)S(1)}, u32[]{:S(2)}, u32[]{:S(2)}) collective-permute-start(f32[4,128,128]{2,1,0:T(8,128)S(1)} %multiply_add_fusion.4), channel_id=1, source_target_pairs={{0,8},{8,16},{16,24},{24,32},{32,40},{40,48},{48,56},{56,64},{64,7... | collective-permute-start | bytes 786440 | tf_op jit(solution)/shard_map/while/body/eval_jaxpr/ppermute | solution.py:13
  183.7 9.7 %collective-permute-start = (f32[4,128,128]{2,1,0:T(8,128)S(1)}, f32[4,128,128]{2,1,0:T(8,128)S(1)}, u32[]{:S(2)}, u32[]{:S(2)}) collective-permute-start(f32[4,128,128]{2,1,0:T(8,128)S(1)} %multiply_add_fusion.4), channel_id=1, source_target_pairs={{0,8},{8,16},{16,24},{24,32},{32,40},{40,48},{48,56},{56,64},{64,7... | collective-permute-start | bytes 786440 | tf_op jit(solution)/shard_map/while/body/eval_jaxpr/ppermute | solution.py:13
  202.8 10.0 %collective-permute-start = (f32[4,128,128]{2,1,0:T(8,128)S(1)}, f32[4,128,128]{2,1,0:T(8,128)S(1)}, u32[]{:S(2)}, u32[]{:S(2)}) collective-permute-start(f32[4,128,128]{2,1,0:T(8,128)S(1)} %multiply_add_fusion.4), channel_id=1, source_target_pairs={{0,8},{8,16},{16,24},{24,32},{32,40},{40,48},{48,56},{56,64},{64,7... | collective-permute-start | bytes 786440 | tf_op jit(solution)/shard_map/while/body/eval_jaxpr/ppermute | solution.py:13
  212.8 11.4 %collective-permute-start = (f32[4,128,128]{2,1,0:T(8,128)S(1)}, f32[4,128,128]{2,1,0:T(8,128)S(1)}, u32[]{:S(2)}, u32[]{:S(2)}) collective-permute-start(f32[4,128,128]{2,1,0:T(8,128)S(1)} %multiply_add_fusion.4), channel_id=1, source_target_pairs={{0,8},{8,16},{16,24},{24,32},{32,40},{40,48},{48,56},{56,64},{64,7... | collective-permute-start | bytes 786440 | tf_op jit(solution)/shard_map/while/body/eval_jaxpr/ppermute | solution.py:13
  224.3 12.8 %collective-permute-start = (f32[4,128,128]{2,1,0:T(8,128)S(1)}, f32[4,128,128]{2,1,0:T(8,128)S(1)}, u32[]{:S(2)}, u32[]{:S(2)}) collective-permute-start(f32[4,128,128]{2,1,0:T(8,128)S(1)} %multiply_add_fusion.4), channel_id=1, source_target_pairs={{0,8},{8,16},{16,24},{24,32},{32,40},{40,48},{48,56},{56,64},{64,7... | collective-permute-start | bytes 786440 | tf_op jit(solution)/shard_map/while/body/eval_jaxpr/ppermute | solution.py:13
  237.2 11.0 %collective-permute-start = (f32[4,128,128]{2,1,0:T(8,128)S(1)}, f32[4,128,128]{2,1,0:T(8,128)S(1)}, u32[]{:S(2)}, u32[]{:S(2)}) collective-permute-start(f32[4,128,128]{2,1,0:T(8,128)S(1)} %multiply_add_fusion.4), channel_id=1, source_target_pairs={{0,8},{8,16},{16,24},{24,32},{32,40},{40,48},{48,56},{56,64},{64,7... | collective-permute-start | bytes 786440 | tf_op jit(solution)/shard_map/while/body/eval_jaxpr/ppermute | solution.py:13
  248.3 9.6 %collective-permute-start = (f32[4,128,128]{2,1,0:T(8,128)S(1)}, f32[4,128,128]{2,1,0:T(8,128)S(1)}, u32[]{:S(2)}, u32[]{:S(2)}) collective-permute-start(f32[4,128,128]{2,1,0:T(8,128)S(1)} %multiply_add_fusion.4), channel_id=1, source_target_pairs={{0,8},{8,16},{16,24},{24,32},{32,40},{40,48},{48,56},{56,64},{64,7... | collective-permute-start | bytes 786440 | tf_op jit(solution)/shard_map/while/body/eval_jaxpr/ppermute | solution.py:13
  266.6 9.5 %collective-permute-start = (f32[4,128,128]{2,1,0:T(8,128)S(1)}, f32[4,128,128]{2,1,0:T(8,128)S(1)}, u32[]{:S(2)}, u32[]{:S(2)}) collective-permute-start(f32[4,128,128]{2,1,0:T(8,128)S(1)} %multiply_add_fusion.4), channel_id=1, source_target_pairs={{0,8},{8,16},{16,24},{24,32},{32,40},{40,48},{48,56},{56,64},{64,7... | collective-permute-start | bytes 786440 | tf_op jit(solution)/shard_map/while/body/eval_jaxpr/ppermute | solution.py:13
  276.2 9.5 %collective-permute-start = (f32[4,128,128]{2,1,0:T(8,128)S(1)}, f32[4,128,128]{2,1,0:T(8,128)S(1)}, u32[]{:S(2)}, u32[]{:S(2)}) collective-permute-start(f32[4,128,128]{2,1,0:T(8,128)S(1)} %multiply_add_fusion.4), channel_id=1, source_target_pairs={{0,8},{8,16},{16,24},{24,32},{32,40},{40,48},{48,56},{56,64},{64,7... | collective-permute-start | bytes 786440 | tf_op jit(solution)/shard_map/while/body/eval_jaxpr/ppermute | solution.py:13
  285.8 9.7 %collective-permute-start = (f32[4,128,128]{2,1,0:T(8,128)S(1)}, f32[4,128,128]{2,1,0:T(8,128)S(1)}, u32[]{:S(2)}, u32[]{:S(2)}) collective-permute-start(f32[4,128,128]{2,1,0:T(8,128)S(1)} %multiply_add_fusion.4), channel_id=1, source_target_pairs={{0,8},{8,16},{16,24},{24,32},{32,40},{40,48},{48,56},{56,64},{64,7... | collective-permute-start | bytes 786440 | tf_op jit(solution)/shard_map/while/body/eval_jaxpr/ppermute | solution.py:13
  304.9 10.0 %collective-permute-start = (f32[4,128,128]{2,1,0:T(8,128)S(1)}, f32[4,128,128]{2,1,0:T(8,128)S(1)}, u32[]{:S(2)}, u32[]{:S(2)}) collective-permute-start(f32[4,128,128]{2,1,0:T(8,128)S(1)} %multiply_add_fusion.4), channel_id=1, source_target_pairs={{0,8},{8,16},{16,24},{24,32},{32,40},{40,48},{48,56},{56,64},{64,7... | collective-permute-start | bytes 786440 | tf_op jit(solution)/shard_map/while/body/eval_jaxpr/ppermute | solution.py:13
  314.9 11.4 %collective-permute-start = (f32[4,128,128]{2,1,0:T(8,128)S(1)}, f32[4,128,128]{2,1,0:T(8,128)S(1)}, u32[]{:S(2)}, u32[]{:S(2)}) collective-permute-start(f32[4,128,128]{2,1,0:T(8,128)S(1)} %multiply_add_fusion.4), channel_id=1, source_target_pairs={{0,8},{8,16},{16,24},{24,32},{32,40},{40,48},{48,56},{56,64},{64,7... | collective-permute-start | bytes 786440 | tf_op jit(solution)/shard_map/while/body/eval_jaxpr/ppermute | solution.py:13
  623.2 109.5 %all-to-all-start.2 = ((bf16[32,8,3,3072]{3,1,2,0:T(8,128)(2,1)}), bf16[32,8,3,3072]{3,1,2,0:T(8,128)(2,1)}, u32[]{:S(2)}, u32[]{:S(2)}) async-start(bf16[32,8,3,3072]{3,1,2,0:T(8,128)(2,1)} %copy.86), calls=%async_computation.3 | async-start | bytes 9437184 | tf_op jit(solution)/shard_map/all_to_all | solution.py:118
  737.0 13.2 %all-to-all-start.3 = ((bf16[8,2,3,3072]{3,1,2,0:T(2,128)(2,1)}), bf16[8,2,3,3072]{3,1,2,0:T(2,128)(2,1)S(1)}, u32[]{:S(2)}, u32[]{:S(2)}) async-start(bf16[8,2,3,3072]{3,1,2,0:T(2,128)(2,1)} %copy.88), calls=%async_computation.4 | async-start | bytes 589824 | tf_op jit(solution)/shard_map/all_to_all | solution.py:126
  (18 other events, 2299.6 us)
Sparse Core Ops, SparseCore 0:
  9.9 85.5 all-gather.1
  331.2 106.2 reduce-scatter.1
where the time goes:
time: 761 us; the launch traced here: 758 us
  waiting for transfers between devices  345 us (45%)
  starting transfers between devices  195 us (26%)
  blocking collectives  128 us (17%)
  local copies, waits for them, and re-layouts  43.6 us (6%)
  matrix products  23.5 us (3%)
  between operations  13.6 us (2%)
  other arithmetic  9.81 us (1%)
    ppermute x31, starting transfers between devices, shifted(): return lax.ppermute(shard, axis, pairs)  182 us
    ppermute x31, waiting for transfers between devices, shifted(): return lax.ppermute(shard, axis, pairs)  129 us
    all_to_all x1, blocking collectives, body(): lax.all_to_all(fanned, 'ctx', split_axis=0, concat_axis=0, tiled=True)  115 us
    reduce_scatter x1, waiting for transfers between devices, body(): lax.psum_scatter(partial_value.astype(jnp.bfloat16), 'ep', scatter_dimens...  106 us
    all_to_all x1, waiting for transfers between devices, body(): lax.all_to_all(partial_out.astype(jnp.bfloat16), 'ctx', split_axis=0, con...  102 us
    convert_element_type x2, local copies, waits for them, and re-layouts, body(): partial_out.astype(jnp.bfloat16)  19 us
  transfers between devices with their start and end apart: 35, of which 34 were waited for; matrix products, arithmetic and copies ran while one was open for 1% of the time, Pallas kernels for 0%

commit v1 on v0

v1 whole, which is shorter than its diff:
```python
import jax
import jax.numpy as jnp
from jax import lax
from jax.experimental import pallas as pl
from jax.experimental.pallas import tpu as pltpu
from jax.sharding import PartitionSpec as P

EPSILON = 1e-06
MESH = pl.DeviceIdType.MESH
F32 = jnp.float32
BF16 = jnp.bfloat16
NY = 4
NZ = 8
NX = 4
DM = 3072
HALF = 1536
SLOTS = 24
CHUNK = 48
SHARD = 96


def place():
    ctx = lax.axis_index("ctx")
    ep = lax.axis_index("ep")
    return ctx // NY, ctx % NY, ep // 2, ep % 2


def at(z, y, x, c):
    return (z * NY + y, x * 2 + c)


def remote(src, dst, send, recv, device):
    return pltpu.make_async_remote_copy(
        src_ref=src,
        dst_ref=dst,
        send_sem=send,
        recv_sem=recv,
        device_id=device,
        device_id_type=MESH,
    )


def await_copy(dst, send, recv, device):
    remote(dst, dst, send, recv, device).wait_recv()


def greet(barrier, devices):
    for device in devices:
        pl.semaphore_signal(barrier, inc=1, device_id=device, device_id_type=MESH)


def nt_dot(a, b):
    return lax.dot_general(a, b, (((1,), (1,)), ((), ())), preferred_element_type=F32)


def tn_dot(a, b):
    return lax.dot_general(a, b, (((0,), (0,)), ((), ())), preferred_element_type=F32)


def dot(a, b):
    return jnp.dot(a, b, preferred_element_type=F32)


def attention_kernel(
    stream_ref,
    query_ref,
    key_ref,
    value_ref,
    rate_ref,
    weight_ref,
    gain_ref,
    routes_ref,
    hidden_ref,
    rows_ref,
    table_ref,
    intra,
    local_out,
    local_in,
    total_out,
    total_in,
    entry,
    state_out,
    state_in,
    proj,
    heads,
    pair_out,
    pair_in,
    part,
    part_out,
    part_in,
    tokens,
    tables,
    s1,
    r1,
    s2,
    r2,
    s3,
    r3,
    wzs,
    wzr,
    wys,
    wyr,
    pair_sem,
    xs,
    xr,
    ts,
    tr,
    cs,
    cr,
):
    z, y, x, c = place()
    up, down = lax.rem(y + 1, NY), lax.rem(y + NY - 1, NY)
    right, left = lax.rem(z + 1, NZ), lax.rem(z + NZ - 1, NZ)
    y_up, y_down = at(z, up, x, c), at(z, down, x, c)
    z_right, z_left = at(right, y, x, c), at(left, y, x, c)
    partner = at(z, y, x, 1 - c)
    barrier = pltpu.get_barrier_semaphore()
    greet(barrier, [at(z, lax.rem(y + d, NY), x, c) for d in range(1, NY)])
    greet(barrier, [at(lax.rem(z + d, NZ), y, x, c) for d in range(1, NZ)])
    greet(barrier, [at(z, y, lax.rem(x + d, NX), c) for d in range(1, NX)])
    greet(barrier, [partner])

    rates = rate_ref[...]
    length = query_ref.shape[0]
    row = lax.broadcasted_iota(jnp.int32, (length, length), 0)
    col = lax.broadcasted_iota(jnp.int32, (length, length), 1)
    gap = (row - col).astype(F32)
    position = lax.broadcasted_iota(jnp.int32, (length, 1), 0).astype(F32)

    def head(ref, h):
        return ref[:, 128 * h : 128 * (h + 1)]

    for h in range(4):
        rate = rates[:, h : h + 1]
        fade = jnp.exp(-rate * (length - 1.0 - position))
        faded = (head(key_ref, h).astype(F32) * fade).astype(BF16)
        local_out[h] = tn_dot(faded, head(value_ref, h)).astype(BF16)
    proj[z * NY + y] = weight_ref[...]
    pl.semaphore_wait(barrier, NY - 1 + NZ - 1 + NX - 1 + 1)

    sends = []

    def launch(copy):
        copy.start()
        sends.append(copy)

    for d in range(1, NY):
        other = lax.rem(y + d, NY)
        launch(remote(local_out.at[other], local_in.at[y], s1.at[d], r1.at[d], at(z, other, x, c)))
    local_in[y] = local_out[y]

    def slot(zz, yy):
        return proj.at[lax.rem(zz + 2 * NZ, NZ) * NY + lax.rem(yy + 2 * NY, NY)]

    def half_slot(zz, yy, half):
        return slot(zz, yy).at[pl.ds(half * 48, 48)]

    def z_step(k):
        if k < 4:
            launch(remote(slot(z - k + 1, y), slot(z - k + 1, y), wzs.at[0, k], wzr.at[0, k], z_right))
            launch(remote(slot(z + k - 1, y), slot(z + k - 1, y), wzs.at[1, k], wzr.at[1, k], z_left))
        else:
            a, b = half_slot(z - 3, y, 0), half_slot(z + 3, y, 1)
            launch(remote(a, a, wzs.at[0, k], wzr.at[0, k], z_right))
            launch(remote(b, b, wzs.at[1, k], wzr.at[1, k], z_left))

    def z_wait(k):
        if k < 4:
            await_copy(slot(z - k, y), wzs.at[0, k], wzr.at[0, k], z_right)
            await_copy(slot(z + k, y), wzs.at[1, k], wzr.at[1, k], z_left)
        else:
            await_copy(half_slot(z + 4, y, 0), wzs.at[0, k], wzr.at[0, k], z_right)
            await_copy(half_slot(z + 4, y, 1), wzs.at[1, k], wzr.at[1, k], z_left)

    def y_send(g):
        s = slot(z + g, y)
        launch(remote(s, s, wys.at[g, 0, 0], wyr.at[g, 0, 0], y_up))
        launch(remote(s, s, wys.at[g, 1, 0], wyr.at[g, 1, 0], y_down))

    def y_relay(g):
        await_copy(slot(z + g, y - 1), wys.at[g, 0, 0], wyr.at[g, 0, 0], y_up)
        a = half_slot(z + g, y - 1, 0)
        launch(remote(a, a, wys.at[g, 0, 1], wyr.at[g, 0, 1], y_up))
        await_copy(slot(z + g, y + 1), wys.at[g, 1, 0], wyr.at[g, 1, 0], y_down)
        b = half_slot(z + g, y + 1, 1)
        launch(remote(b, b, wys.at[g, 1, 1], wyr.at[g, 1, 1], y_down))

    def y_finish(g):
        await_copy(half_slot(z + g, y + 2, 0), wys.at[g, 0, 1], wyr.at[g, 0, 1], y_up)
        await_copy(half_slot(z + g, y + 2, 1), wys.at[g, 1, 1], wyr.at[g, 1, 1], y_down)

    z_step(1)
    y_send(0)

    for h in range(4):
        rate = rates[:, h : h + 1]
        decay = jnp.where(gap >= 0, jnp.exp(-rate * jnp.maximum(gap, 0.0)), 0.0)
        scores = nt_dot(head(query_ref, h), head(key_ref, h))
        intra[h] = dot((scores * decay).astype(BF16), head(value_ref, h))

    for d in range(1, NY):
        other = lax.rem(y + d, NY)
        await_copy(local_in.at[lax.rem(y + NY - d, NY)], s1.at[d], r1.at[d], at(z, other, x, c))
    lane = lax.broadcasted_iota(jnp.int32, rates.shape, 1)
    own_rate = jnp.sum(jnp.where(lane == y, rates, 0.0), axis=1, keepdims=True)

    def power(n):
        return jnp.exp(-own_rate * (128.0 * n))

    locals_in = [local_in[i].astype(F32) for i in range(NY)]
    total = locals_in[3]
    for i in range(3):
        total = total + power(3 - i) * locals_in[i]
    total_out[...] = total.astype(BF16)
    for d in range(1, NZ):

        @pl.when(z + d < NZ)
        def _(d=d):
            remote(
                total_out, total_in.at[z], s2.at[d], r2.at[d], at(lax.rem(z + d, NZ), y, x, c)
            ).start()

    z_wait(1)
    z_step(2)
    y_send(1)
    y_send(7)
    y_relay(0)

    entry[...] = jnp.zeros_like(entry)
    for d in range(1, NZ):

        @pl.when(z >= d)
        def _(d=d):
            source = lax.rem(z + NZ - d, NZ)
            await_copy(total_in.at[source], s2.at[d], r2.at[d], at(source, y, x, c))
            entry[...] += power(4 * (d - 1)) * total_in[source].astype(F32)

    incoming = entry[...]
    for i in range(NY):
        state_out[i] = incoming.astype(BF16)
        incoming = power(1) * incoming + locals_in[i]
    for d in range(1, NY):
        other = lax.rem(y + d, NY)
        launch(remote(state_out.at[other], state_in.at[y], s3.at[d], r3.at[d], at(z, other, x, c)))
    state_in[y] = state_out[y]

    z_wait(2)
    z_step(3)
    y_send(2)
    y_send(6)
    y_relay(1)
    y_relay(7)

    for d in range(1, NY):
        other = lax.rem(y + d, NY)
        await_copy(state_in.at[lax.rem(y + NY - d, NY)], s3.at[d], r3.at[d], at(z, other, x, c))
    for h in range(4):
        rate = rates[:, h : h + 1]
        fade = jnp.exp(-rate * (position + 1.0))
        mixed = intra[h] + fade * dot(head(query_ref, h), state_in[h])
        mean = jnp.mean(mixed * mixed, axis=-1, keepdims=True)
        out = (mixed * lax.rsqrt(mean + EPSILON)).astype(BF16)
        for e in range(8):
            heads[e // 2, e % 2, :, 128 * h : 128 * (h + 1)] = out[16 * e : 16 * (e + 1)]

    z_wait(3)
    z_step(4)
    y_send(3)
    y_send(5)
    y_relay(2)
    y_relay(6)
    z_wait(4)
    y_send(4)
    y_relay(3)
    y_relay(5)
    y_relay(4)
    for g in range(NZ):
        y_finish(g)

    def project(core, store):
        lhs = heads[:, core].reshape(64, 512)
        for n in range(4):
            rhs = proj[8 * n : 8 * (n + 1)].reshape(8 * SHARD, 512)
            store(n, nt_dot(lhs, rhs))

    def store_pair(n, value):
        pair_out[:, :, 768 * n : 768 * (n + 1)] = value.astype(BF16).reshape(4, 16, 768)

    project(1 - c, store_pair)
    pair_copy = remote(pair_out, pair_in, pair_sem.at[0], pair_sem.at[1], partner)
    launch(pair_copy)

    def store_part(n, value):
        part[:, :, 768 * n : 768 * (n + 1)] = value.reshape(4, 16, 768)

    project(c, store_part)
    pair_copy.wait_recv()
    part[...] += pair_in[...].astype(F32)
    part_out[...] = part[...].astype(BF16)
    for d in (2, 1, 3):
        other = lax.rem(x + d, NX)
        launch(remote(part_out.at[other], part_in.at[x], xs.at[d], xr.at[d], at(z, y, other, c)))
    hidden = stream_ref[...].astype(F32) + part[x]
    for d in (1, 3, 2):
        source = lax.rem(x + NX - d, NX)
        await_copy(part_in.at[source], xs.at[d], xr.at[d], at(z, y, source, c))
        hidden = hidden + part_in[source].astype(F32)
    hidden_ref[...] = hidden
    mean = jnp.mean(hidden * hidden, axis=-1, keepdims=True)
    tokens[x, c] = (hidden * lax.rsqrt(mean + EPSILON) * gain_ref[...]).astype(BF16)
    tables[x, c] = routes_ref[...]
    for d in (2, 1, 3):
        other = lax.rem(x + d, NX)
        device = at(z, y, other, c)
        launch(remote(tokens.at[x, c], tokens.at[x, c], ts.at[0, d], tr.at[0, d], device))
        launch(remote(tables.at[x, c], tables.at[x, c], ts.at[1, d], tr.at[1, d], device))
    for d in (0, 1, 3, 2):
        source = lax.rem(x + NX - d, NX)
        if d:
            device = at(z, y, source, c)
            await_copy(tokens.at[source, c], ts.at[0, d], tr.at[0, d], device)
            await_copy(tables.at[source, c], ts.at[1, d], tr.at[1, d], device)
        launch(remote(tokens.at[source, c], tokens.at[source, c], cs.at[0, d], cr.at[0, d], partner))
        launch(remote(tables.at[source, c], tables.at[source, c], cs.at[1, d], cr.at[1, d], partner))
    for d in (0, 1, 3, 2):
        source = lax.rem(x + NX - d, NX)
        await_copy(tokens.at[source, 1 - c], cs.at[0, d], cr.at[0, d], partner)
        await_copy(tables.at[source, 1 - c], cs.at[1, d], cr.at[1, d], partner)
    rows_ref[...] = tokens[...].reshape(128, DM)
    table_ref[...] = tables[...].reshape(128, 128)
    for d in range(1, NZ):

        @pl.when(z + d < NZ)
        def _(d=d):
            remote(
                total_out, total_in.at[z], s2.at[d], r2.at[d], at(lax.rem(z + d, NZ), y, x, c)
            ).wait_send()

    for copy in sends:
        copy.wait_send()


def expert_kernel(
    hidden_ref,
    rows_ref,
    table_ref,
    router_ref,
    gate_hbm,
    up_hbm,
    down_hbm,
    out_ref,
    gate,
    up,
    down,
    picked,
    cross_out,
    flat,
    part,
    first_up,
    first_down,
    second_up,
    second_down,
    total,
    line_out,
    line_in,
    back_out,
    back_in,
    mixed,
    pair_out,
    pair_in,
    home_out,
    home_in,
    wsem,
    dxs,
    dxr,
    dzs,
    dzr,
    dys,
    dyr,
    eys,
    eyr,
    ezs,
    ezr,
    bs,
    br,
    ps,
    pr,
    xs,
    xr,
):
    z, y, x, c = place()
    half, zl = z // 4, z % 4
    up_y, down_y = lax.rem(y + 1, NY), lax.rem(y + NY - 1, NY)
    far_y = lax.rem(y + 2, NY)
    y_up, y_down = at(z, up_y, x, c), at(z, down_y, x, c)
    z_right = at(lax.rem(z + 1, NZ), y, x, c)
    z_left = at(lax.rem(z + NZ - 1, NZ), y, x, c)
    mirror = at(NZ - 1 - z, y, x, c)
    partner = at(z, y, x, 1 - c)
    barrier = pltpu.get_barrier_semaphore()
    greet(barrier, [y_up, y_down, partner])
    greet(barrier, [at(lax.rem(z + d, NZ), y, x, c) for d in range(1, NZ)])
    greet(barrier, [at(z, y, lax.rem(x + d, NX), c) for d in range(1, NX)])
    loads = [
        pltpu.make_async_copy(gate_hbm, gate, wsem.at[0]),
        pltpu.make_async_copy(up_hbm, up, wsem.at[1]),
        pltpu.make_async_copy(down_hbm, down, wsem.at[2]),
    ]
    for load in loads:
        load.start()
    sends = []

    def launch(copy):
        copy.start()
        sends.append(copy)

    first = table_ref[:, 0:1]
    second = table_ref[:, 1:2]
    group = x * 2 + c
    lane = lax.broadcasted_iota(jnp.int32, (128, 128), 1)
    earlier = (lane < lax.broadcasted_iota(jnp.int32, (128, 128), 0)).astype(BF16)

    def select(which):
        expert = group * 2 + which
        hit = jnp.logical_or(first == expert, second == expert)
        wide = jnp.broadcast_to(jnp.where(hit, 1.0, 0.0), (128, 128))
        rank = dot(earlier, wide.astype(BF16)).astype(jnp.int32)
        low = jnp.where(rank == lane, wide, 0.0)[:, :CHUNK]
        high = jnp.where(rank == lane - SLOTS, wide, 0.0)[:, :CHUNK]
        keep = lax.broadcasted_iota(jnp.int32, (128, CHUNK), 1) < SLOTS
        return jnp.where(keep, low, 0.0).astype(BF16), jnp.where(keep, 0.0, high).astype(BF16)

    def pick(which):
        low, high = select(which)
        return (tn_dot(low, rows_ref[:, :HALF]) + tn_dot(high, rows_ref[:, HALF:])).astype(BF16)

    cross_out[...] = pick(1 - half)
    picked[z * NY + y] = pick(half)
    pl.semaphore_wait(barrier, 3 + NZ - 1 + NX - 1)
    here = picked.at[z * NY + y]
    launch(remote(cross_out, here, dxs, dxr, mirror))

    order = [zl, zl + 1 - 2 * (zl % 2), 2 - zl // 2, 3 - 3 * (zl // 2)]

    def z_index(p, e):
        own = half * 4 + p
        return own if e == 0 else NZ - 1 - own

    def slot(zz, yy):
        return picked.at[zz * NY + yy]

    def lanes(ref, which):
        return ref.at[:, pl.ds(which * 768, 768)]

    def forward(p, e):
        s = slot(z_index(p, e), y)
        return (
            remote(s, s, dzs.at[0, p, e], dzr.at[p, e], z_right),
            remote(s, s, dzs.at[1, p, e], dzr.at[p, e], z_left),
        )

    def spread(i, e):
        p = order[i]
        zz = z_index(p, e)
        s = slot(zz, y)
        if i > 0:
            await_copy(s, dzs.at[0, p, e], dzr.at[p, e], z_right)
        elif e == 1:
            await_copy(s, dxs, dxr, mirror)

        @pl.when(jnp.logical_and(p <= zl, zl < 3))
        def _():
            forward(p, e)[0].start()

        @pl.when(jnp.logical_and(p >= zl, zl > 0))
        def _():
            forward(p, e)[1].start()

        launch(remote(s, s, dys.at[zz, 0, 0], dyr.at[zz, 0, 0], y_up))
        launch(remote(s, s, dys.at[zz, 1, 0], dyr.at[zz, 1, 0], y_down))

    def relay(i, e):
        zz = z_index(order[i], e)
        await_copy(slot(zz, down_y), dys.at[zz, 0, 0], dyr.at[zz, 0, 0], y_up)
        a = lanes(slot(zz, down_y), 0)
        launch(remote(a, a, dys.at[zz, 0, 1], dyr.at[zz, 0, 1], y_up))
        await_copy(slot(zz, up_y), dys.at[zz, 1, 0], dyr.at[zz, 1, 0], y_down)
        b = lanes(slot(zz, up_y), 1)
        launch(remote(b, b, dys.at[zz, 1, 1], dyr.at[zz, 1, 1], y_down))

    def finish(i, e):
        zz = z_index(order[i], e)
        await_copy(lanes(slot(zz, far_y), 0), dys.at[zz, 0, 1], dyr.at[zz, 0, 1], y_up)
        await_copy(lanes(slot(zz, far_y), 1), dys.at[zz, 1, 1], dyr.at[zz, 1, 1], y_down)

    sequence = [(0, 0), (1, 0), (0, 1), (2, 0), (1, 1), (3, 0), (2, 1), (3, 1)]
    for n, (i, e) in enumerate(sequence):
        spread(i, e)
        if n >= 1:
            relay(*sequence[n - 1])
    relay(*sequence[-1])
    for i, e in sequence:
        finish(i, e)

    def flatten(n, carry):
        a = picked[2 * n].astype(F32)
        b = picked[2 * n + 1].astype(F32)
        rows = pl.ds(pl.multiple_of(n * CHUNK, CHUNK), CHUNK)
        flat[rows, :HALF] = jnp.concatenate([a[:SLOTS], b[:SLOTS]], axis=0).astype(BF16)
        flat[rows, HALF:] = jnp.concatenate([a[SLOTS:], b[SLOTS:]], axis=0).astype(BF16)
        return carry

    lax.fori_loop(0, 16, flatten, 0)
    for load in loads:
        load.wait()

    def compute(m, carry):
        rows = flat[pl.ds(pl.multiple_of(m * 192, 192), 192), :]
        gated = dot(rows, gate[...])
        inner = (gated * jax.nn.sigmoid(gated) * dot(rows, up[...])).astype(BF16)
        for side in range(2):
            result = dot(inner, down[:, HALF * side : HALF * (side + 1)])
            if side == 0:
                kept = result
            else:
                for i in range(8):
                    block = slice(SLOTS * i, SLOTS * (i + 1))
                    part[m * 8 + i] = jnp.concatenate([kept[block], result[block]], axis=0).astype(BF16)
        return carry

    lax.fori_loop(0, 4, compute, 0)

    def mine(zz, yy):
        return part.at[zz * NY + yy]

    groups = [(i, e) for i in (3, 2, 1, 0) for e in (0, 1)]
    for i, e in groups:
        zz = z_index(order[i], e)
        launch(remote(lanes(mine(zz, far_y), 0), first_up.at[zz], eys.at[zz, 0, 0], eyr.at[zz, 0, 0], y_up))
        launch(remote(lanes(mine(zz, far_y), 1), first_down.at[zz], eys.at[zz, 1, 0], eyr.at[zz, 1, 0], y_down))

    def pass_on(i, e):
        zz = z_index(order[i], e)
        await_copy(first_up.at[zz], eys.at[zz, 0, 0], eyr.at[zz, 0, 0], y_up)
        a = zz * NY + up_y
        part[a, :, :768] = (part[a, :, :768].astype(F32) + first_up[zz].astype(F32)).astype(BF16)
        launch(remote(part.at[a], second_up.at[zz], eys.at[zz, 0, 1], eyr.at[zz, 0, 1], y_up))
        await_copy(first_down.at[zz], eys.at[zz, 1, 0], eyr.at[zz, 1, 0], y_down)
        b = zz * NY + down_y
        part[b, :, 768:] = (part[b, :, 768:].astype(F32) + first_down[zz].astype(F32)).astype(BF16)
        launch(remote(part.at[b], second_down.at[zz], eys.at[zz, 1, 1], eyr.at[zz, 1, 1], y_down))

    def collect(i, e):
        zz = z_index(order[i], e)
        await_copy(second_up.at[zz], eys.at[zz, 0, 1], eyr.at[zz, 0, 1], y_up)
        await_copy(second_down.at[zz], eys.at[zz, 1, 1], eyr.at[zz, 1, 1], y_down)
        total[zz] = (
            part[zz * NY + y].astype(F32)
            + second_up[zz].astype(F32)
            + second_down[zz].astype(F32)
        )

    def line_copy(p, e, side):
        return remote(
            line_out.at[p, e],
            line_in.at[side, p, e],
            ezs.at[p, e],
            ezr.at[side, p, e],
            z_right if side == 0 else z_left,
        )

    def along(i, e):
        p = order[i]
        zz = z_index(p, e)

        @pl.when(jnp.logical_and(p > zl, zl > 0))
        def _():
            await_copy(line_in.at[0, p, e], ezs.at[p, e], ezr.at[0, p, e], z_left)
            total[zz] += line_in[0, p, e].astype(F32)

        @pl.when(jnp.logical_and(p < zl, zl < 3))
        def _():
            await_copy(line_in.at[1, p, e], ezs.at[p, e], ezr.at[1, p, e], z_right)
            total[zz] += line_in[1, p, e].astype(F32)

        line_out[p, e] = total[zz].astype(BF16)

        @pl.when(p > zl)
        def _():
            line_copy(p, e, 0).start()

        @pl.when(p < zl)
        def _():
            line_copy(p, e, 1).start()

    def arrive(e):
        zz = z_index(zl, e)

        @pl.when(zl > 0)
        def _():
            await_copy(line_in.at[0, zl, e], ezs.at[zl, e], ezr.at[0, zl, e], z_left)
            total[zz] += line_in[0, zl, e].astype(F32)

        @pl.when(zl < 3)
        def _():
            await_copy(line_in.at[1, zl, e], ezs.at[zl, e], ezr.at[1, zl, e], z_right)
            total[zz] += line_in[1, zl, e].astype(F32)

    for n in range(10):
        if n < 8:
            pass_on(*groups[n])
        if n >= 2:
            collect(*groups[n - 2])
            if groups[n - 2][0] > 0:
                along(*groups[n - 2])
    arrive(1)
    back_out[1] = total[z_index(zl, 1)].astype(BF16)
    launch(remote(back_out.at[1], back_in, bs, br, mirror))
    arrive(0)
    back_out[0] = total[z_index(zl, 0)].astype(BF16)

    logits = dot(rows_ref[...], router_ref[...])
    expert = lax.broadcasted_iota(jnp.int32, logits.shape, 1)
    lift_first = jax.nn.sigmoid(jnp.sum(jnp.where(expert == first, logits, 0.0), axis=1, keepdims=True))
    lift_second = jax.nn.sigmoid(jnp.sum(jnp.where(expert == second, logits, 0.0), axis=1, keepdims=True))
    both = lift_first + lift_second
    share_first, share_second = lift_first / both, lift_second / both

    def contribution(which, returned):
        chosen = group * 2 + which
        share = jnp.where(first == chosen, share_first, 0.0) + jnp.where(
            second == chosen, share_second, 0.0
        )
        low, high = select(which)
        return share * dot(low, returned), share * dot(high, returned)

    low, high = contribution(half, back_out[0])
    await_copy(back_in, bs, br, mirror)
    far_low, far_high = contribution(1 - half, back_in[...])
    mixed[:, :, :, :HALF] = (low + far_low).reshape(4, 2, 16, HALF)
    mixed[:, :, :, HALF:] = (high + far_high).reshape(4, 2, 16, HALF)
    pair_out[...] = mixed[:, 1 - c].astype(BF16)
    pair_copy = remote(pair_out, pair_in, ps, pr, partner)
    launch(pair_copy)
    pair_copy.wait_recv()
    summed = mixed[:, c] + pair_in[...].astype(F32)
    mixed[:, c] = summed
    home_out[...] = summed.astype(BF16)
    for d in (2, 1, 3):
        other = lax.rem(x + d, NX)
        launch(remote(home_out.at[other], home_in.at[x], xs.at[d], xr.at[d], at(z, y, other, c)))
    result = hidden_ref[...] + mixed[x, c]
    for d in (1, 3, 2):
        source = lax.rem(x + NX - d, NX)
        await_copy(home_in.at[source], xs.at[d], xr.at[d], at(z, y, source, c))
        result = result + home_in[source].astype(F32)
    out_ref[...] = result.astype(BF16)

    for i in range(4):
        for e in range(2):
            p = order[i]

            @pl.when(jnp.logical_and(p <= zl, zl < 3))
            def _(p=p, e=e):
                forward(p, e)[0].wait_send()

            @pl.when(jnp.logical_and(p >= zl, zl > 0))
            def _(p=p, e=e):
                forward(p, e)[1].wait_send()

            if i > 0:

                @pl.when(p > zl)
                def _(p=p, e=e):
                    line_copy(p, e, 0).wait_send()

                @pl.when(p < zl)
                def _(p=p, e=e):
                    line_copy(p, e, 1).wait_send()

    for copy in sends:
        copy.wait_send()


VMEM = pl.BlockSpec(memory_space=pltpu.VMEM)
ANY = pl.BlockSpec(memory_space=pl.ANY)
DMA = pltpu.SemaphoreType.DMA
LIMIT = 56 * 2**20


def attention_call(*operands):
    bf = lambda *shape: pltpu.VMEM(shape, BF16)
    fl = lambda *shape: pltpu.VMEM(shape, F32)
    return pl.pallas_call(
        attention_kernel,
        out_shape=(
            jax.ShapeDtypeStruct((16, DM), F32),
            jax.ShapeDtypeStruct((128, DM), BF16),
            jax.ShapeDtypeStruct((128, 128), jnp.int32),
        ),
        in_specs=[VMEM] * 8,
        out_specs=(VMEM, VMEM, VMEM),
        scratch_shapes=[
            fl(4, 128, 128),
            bf(4, 128, 128),
            bf(4, 128, 128),
            bf(128, 128),
            bf(8, 128, 128),
            fl(128, 128),
            bf(4, 128, 128),
            bf(4, 128, 128),
            bf(32, SHARD, 512),
            bf(4, 2, 16, 512),
            bf(4, 16, DM),
            bf(4, 16, DM),
            fl(4, 16, DM),
            bf(4, 16, DM),
            bf(4, 16, DM),
            bf(4, 2, 16, DM),
            pltpu.VMEM((4, 2, 16, 128), jnp.int32),
            DMA((4,)),
            DMA((4,)),
            DMA((8,)),
            DMA((8,)),
            DMA((4,)),
            DMA((4,)),
            DMA((2, 5)),
            DMA((2, 5)),
            DMA((8, 2, 2)),
            DMA((8, 2, 2)),
            DMA((2,)),
            DMA((4,)),
            DMA((4,)),
            DMA((2, 4)),
            DMA((2, 4)),
            DMA((2, 4)),
            DMA((2, 4)),
        ],
        compiler_params=pltpu.CompilerParams(
            collective_id=0, has_side_effects=True, vmem_limit_bytes=LIMIT
        ),
        name="attend",
    )(*operands)


def expert_call(*operands):
    bf = lambda *shape: pltpu.VMEM(shape, BF16)
    fl = lambda *shape: pltpu.VMEM(shape, F32)
    return pl.pallas_call(
        expert_kernel,
        out_shape=jax.ShapeDtypeStruct((16, DM), BF16),
        in_specs=[VMEM] * 4 + [ANY] * 3,
        out_specs=VMEM,
        scratch_shapes=[
            bf(DM, 288),
            bf(DM, 288),
            bf(288, DM),
            bf(32, CHUNK, HALF),
            bf(CHUNK, HALF),
            bf(768, DM),
            bf(32, CHUNK, HALF),
            bf(8, CHUNK, 768),
            bf(8, CHUNK, 768),
            bf(8, CHUNK, HALF),
            bf(8, CHUNK, HALF),
            fl(8, CHUNK, HALF),
            bf(4, 2, CHUNK, HALF),
            bf(2, 4, 2, CHUNK, HALF),
            bf(2, CHUNK, HALF),
            bf(CHUNK, HALF),
            fl(4, 2, 16, DM),
            bf(4, 16, DM),
            bf(4, 16, DM),
            bf(4, 16, DM),
            bf(4, 16, DM),
            DMA((3,)),
            DMA,
            DMA,
            DMA((2, 4, 2)),
            DMA((4, 2)),
            DMA((8, 2, 2)),
            DMA((8, 2, 2)),
            DMA((8, 2, 2)),
            DMA((8, 2, 2)),
            DMA((4, 2)),
            DMA((2, 4, 2)),
            DMA,
            DMA,
            DMA,
            DMA,
            DMA((4,)),
            DMA((4,)),
        ],
        compiler_params=pltpu.CompilerParams(
            collective_id=1, has_side_effects=True, vmem_limit_bytes=LIMIT
        ),
        name="experts",
    )(*operands)


def body(
    stream,
    query,
    key,
    value,
    decay_rate,
    out_weight,
    norm_gain,
    router_weight,
    routes,
    expert_gate,
    expert_up,
    expert_down,
):
    wide_routes = jnp.pad(routes, ((0, 0), (0, 126)))
    hidden, rows, table = attention_call(
        stream,
        query,
        key,
        value,
        decay_rate.reshape(1, 4),
        out_weight.T,
        norm_gain.reshape(1, DM),
        wide_routes,
    )
    return expert_call(hidden, rows, table, router_weight, expert_gate, expert_up, expert_down)


def solution(mesh):
    placed = (
        P(("ctx", "ep"), None),
        P("ctx", "ep"),
        P("ctx", "ep"),
        P("ctx", "ep"),
        P("ep"),
        P("ep", "ctx"),
        P(),
        P(),
        P(("ctx", "ep"), None),
        P(None, ("ep", "ctx")),
        P(None, ("ep", "ctx")),
        P(("ep", "ctx"), None),
    )
    return jax.shard_map(
        body, mesh=mesh, in_specs=placed, out_specs=P(("ctx", "ep"), None), check_vma=False
    )
```

time: 761 us -> 194 us (0.25)
  waiting for transfers between devices: 345 us -> 0 us
  starting transfers between devices: 195 us -> 0 us
  Pallas kernels: 0 us -> 183 us
  blocking collectives: 128 us -> 0 us
  local copies, waits for them, and re-layouts: 43.6 us -> 11.6 us
  matrix products: 23.5 us -> 0 us
  between operations: 13.6 us -> 0.03 us
  other arithmetic: 9.81 us -> 0 us
    pallas_call x0 -> x2, Pallas kernels: none -> 183 us  [the longest x1 119 us: expert_call(): pl.pallas_call(expert_kernel, out_shape=jax.ShapeDtypeStruct((16, DM), BF...]
    ppermute x31 -> x0, starting transfers between devices: 182 us -> none  [shifted(): return lax.ppermute(shard, axis, pairs)]
    ppermute x31 -> x0, waiting for transfers between devices: 129 us -> none  [shifted(): return lax.ppermute(shard, axis, pairs)]
    all_to_all x2 -> x0, blocking collectives: 128 us -> none  [the longest x1 115 us: body(): lax.all_to_all(fanned, 'ctx', split_axis=0, concat_axis=0, tiled=True)]
    all_to_all x2 -> x0, waiting for transfers between devices: 109 us -> none  [the longest x1 102 us: body(): lax.all_to_all(partial_out.astype(jnp.bfloat16), 'ctx', split_axis=0, con...]
    reduce_scatter x1 -> x0, waiting for transfers between devices: 106 us -> none  [body(): lax.psum_scatter(partial_value.astype(jnp.bfloat16), 'ep', scatter_dimens...]
    dot_general x9 -> x0, matrix products: 23.5 us -> none  [the longest x1 10.4 us: body(): jnp.dot(inner_act, expert_down, preferred_element_type=jnp.float32)]
    convert_element_type x3 -> x0, local copies, waits for them, and re-layouts: 20 us -> none  [the longest x2 19 us: body(): partial_out.astype(jnp.bfloat16)]
  transfers between devices with their start and end apart: 35 -> 0, of which waited for: 34 -> 0; matrix products, arithmetic and copies ran while one was open for 1% -> 0% of each run, Pallas kernels for 0% -> 0%
where the time goes in v1:
time: 194 us
  Pallas kernels  183 us (94%)
  local copies, waits for them, and re-layouts  11.6 us (6%)
    pallas_call x1, Pallas kernels, expert_call(): pl.pallas_call(expert_kernel, out_shape=jax.ShapeDtypeStruct((16, DM), BF...  119 us
    pallas_call x1, Pallas kernels, attention_call(): pl.pallas_call(attention_kernel, out_shape=(jax.ShapeDtypeStruct((16, DM)...  63.6 us
    unnamed x7, local copies, waits for them, and re-layouts  11 us

profile of v1, /device:TPU:1, one launch (start us, length us, event | category | flops | bytes accessed | tf_op | source)
XLA Modules:
  0.0 194.2 jit_solution(3350763554515439588)
XLA Ops:
  0.0 0.8 copy.13
  0.8 0.6 pad.4.routes_ref
  1.4 2.1 %copy.14.router_ref = bf16[3072,16]{1,0:T(8,128)(2,1)} copy(bf16[3072,16]{0,1:T(8,128)(2,1)} %param.19) | data formatting | bytes 196608 | tf_op args[7]
  3.5 63.6 %attend.1 = (f32[16,3072]{1,0:T(8,128)}, bf16[128,3072]{1,0:T(8,128)(2,1)}, s32[128,128]{1,0:T(8,128)}) custom-call(bf16[16,3072]{1,0:T(8,128)(2,1)} %stream_ref.1, bf16[128,512]{1,0:T(8,128)(2,1)} %query_ref.1, bf16[128,512]{1,0:T(8,128)(2,1)} %key_ref.1, bf16[128,512]{1,0:T(8,128)(2,1)} %value_ref.1, f32[1,4]{1,0:T(1,128)} %bitcast.5, ...), custom_call_target="tpu_custom_call" | custom-call | tf_op jit(solution)/shard_map/attend/pallas_call | solution.py:694
  67.0 0.0 copy-start
  67.0 4.1 %copy.15.gate_hbm = bf16[3072,288]{1,0:T(8,128)(2,1)} copy(bf16[3072,288]{0,1:T(8,128)(2,1)} %param.21) | data formatting | bytes 3538944 | tf_op args[9]
  71.2 0.0 copy-done
  71.2 2.4 %copy.16.up_hbm = bf16[3072,288]{1,0:T(8,128)(2,1)} copy(bf16[3072,288]{0,1:T(8,128)(2,1)S(1)} %copy-done) | data formatting | bytes 3538944 | tf_op args[10]
  73.6 119.0 %experts.1 = bf16[16,3072]{1,0:T(8,128)(2,1)} custom-call(f32[16,3072]{1,0:T(8,128)} %get-tuple-element.8.hidden_ref, bf16[128,3072]{1,0:T(8,128)(2,1)} %get-tuple-element.9.rows_ref, s32[128,128]{1,0:T(8,128)} %get-tuple-element.10.table_ref, bf16[3072,16]{1,0:T(8,128)(2,1)} %copy.14.router_ref, bf16[3072,288]{1,0:T(8,128)(2,1)} %copy.15.gate_hbm, ...), custom_call_target="tpu_custom_call" | custom-call | tf_op jit(solution)/shard_map/experts/pallas_call | solution.py:749
  192.6 1.5 copy.18
Async XLA Ops:
  67.0 4.2 %copy-start = (bf16[3072,288]{0,1:T(8,128)(2,1)S(1)}, bf16[3072,288]{0,1:T(8,128)(2,1)}, u32[]{:S(2)}) copy-start(bf16[3072,288]{0,1:T(8,128)(2,1)} %param.22) | copy-start | bytes 5308420

commit v2 on v0

v2 whole, which is shorter than its diff:
```python
import jax
import jax.numpy as jnp
from jax import lax
from jax.experimental import pallas as pl
from jax.experimental.pallas import tpu as pltpu
from jax.sharding import PartitionSpec as P

EPSILON = 1e-06
MESH = pl.DeviceIdType.MESH
F32 = jnp.float32
BF16 = jnp.bfloat16
NY = 4
NZ = 8
NX = 4
DM = 3072
HALF = 1536
SLOTS = 24
CHUNK = 48
SHARD = 96
HIDDEN = 288
PIECE = 144


def bf(*shape):
    return pltpu.VMEM(shape, BF16)


def fl(*shape):
    return pltpu.VMEM(shape, F32)


def dma(*shape):
    return pltpu.SemaphoreType.DMA(shape)


INPUTS = (
    "stream", "query", "key", "value", "rates", "weight", "gain", "routes", "router",
    "gate_hbm", "up_hbm", "down_hbm", "out",
)
SCRATCH = dict(
    intra=fl(4, 128, 128),
    local_out=bf(4, 128, 128),
    local_in=bf(4, 128, 128),
    total_out=bf(128, 128),
    total_in=bf(8, 128, 128),
    entry=fl(128, 128),
    state_out=bf(4, 128, 128),
    state_in=bf(4, 128, 128),
    proj=bf(8, SHARD, 512),
    heads=bf(4, 4, 2, 16, 512),
    pair_out=bf(4, 4, 16, 768),
    pair_in=bf(4, 4, 16, 768),
    part=fl(4, 4, 16, 768),
    part_out=bf(4, 4, 16, 768),
    part_in=bf(4, 4, 16, 768),
    slab=fl(4, 16, 768),
    slab_out=bf(4, 16, 768),
    slab_in=bf(4, 16, 768),
    hidden=fl(16, DM),
    tokens=bf(4, 2, 16, DM),
    tables=pltpu.VMEM((4, 2, 16, 128), jnp.int32),
    gate=bf(2 * HIDDEN, DM),
    up=bf(2 * HIDDEN, DM),
    down=bf(2 * HIDDEN, DM),
    sel=bf(2, 2, 2, 128, CHUNK),
    share=fl(2, 2, 128, 128),
    cross=bf(2, CHUNK, HALF),
    line=bf(2, 4, CHUNK, HALF),
    got=bf(3, 4, CHUNK, HALF),
    flat=bf(192, DM),
    partial=bf(4, 4, CHUNK, HALF),
    back=bf(3, 4, CHUNK, HALF),
    total=fl(2, 4, CHUNK, HALF),
    line_out=bf(2, 4, CHUNK, HALF),
    line_in=bf(2, 2, 4, CHUNK, HALF),
    final=bf(2, CHUNK, HALF),
    ret=bf(2, CHUNK, HALF),
    mixed=fl(4, 2, 16, DM),
    home_out=bf(4, 2, 16, DM),
    home_in=bf(4, 16, DM),
    home=fl(16, DM),
    load_sem=dma(3),
    local_s=dma(4), local_r=dma(4),
    total_s=dma(8), total_r=dma(8),
    state_s=dma(4), state_r=dma(4),
    proj_s=dma(2, 5), proj_r=dma(2, 5),
    heads_s=dma(4), heads_r=dma(4),
    pair_s=dma(1), pair_r=dma(1),
    part_s=dma(4), part_r=dma(4),
    slab_s=dma(4), slab_r=dma(4),
    tok_s=dma(2, 4), tok_r=dma(2, 4, 2),
    own_s=dma(3), own_r=dma(3),
    swap_s=dma(3, 2), swap_r=dma(3, 2),
    pass_s=dma(3, 2), pass_r=dma(3, 2),
    cross_s=dma(2), cross_r=dma(2),
    line_s=dma(2, 2, 4), line_r=dma(2, 4),
    got_s=dma(3, 4), got_r=dma(3, 4),
    back_s=dma(3, 4), back_r=dma(3, 4),
    sum_s=dma(2, 4), sum_r=dma(2, 2, 4),
    ret_s=dma(2), ret_r=dma(2),
    home_s=dma(4, 2), home_r=dma(4),
)


class Refs:
    def __init__(self, refs):
        for name, ref in zip(INPUTS + tuple(SCRATCH), refs, strict=True):
            setattr(self, name, ref)


def at(z, y, x, c):
    return (z * NY + y, x * 2 + c)


def remote(src, dst, send, recv, device):
    return pltpu.make_async_remote_copy(
        src_ref=src,
        dst_ref=dst,
        send_sem=send,
        recv_sem=recv,
        device_id=device,
        device_id_type=MESH,
    )


def await_copy(dst, send, recv, device):
    remote(dst, dst, send, recv, device).wait_recv()


def greet(barrier, devices):
    for device in devices:
        pl.semaphore_signal(barrier, inc=1, device_id=device, device_id_type=MESH)


def nt_dot(a, b):
    return lax.dot_general(a, b, (((1,), (1,)), ((), ())), preferred_element_type=F32)


def tn_dot(a, b):
    return lax.dot_general(a, b, (((0,), (0,)), ((), ())), preferred_element_type=F32)


def dot(a, b):
    return jnp.dot(a, b, preferred_element_type=F32)


def kernel(*refs):
    r = Refs(refs)
    ctx = lax.axis_index("ctx")
    ep = lax.axis_index("ep")
    z, y, x, c = ctx // NY, ctx % NY, ep // 2, ep % 2
    half, zl = z // 4, z % 4
    role = y % 2
    source = z % 2 == c
    keeper = c == role
    core = z % 2

    def ring_y(d):
        return lax.rem(y + d + NY, NY)

    def ring_z(d):
        return lax.rem(z + d + NZ, NZ)

    def ring_x(d):
        return lax.rem(x + d + NX, NX)

    def on_y(d):
        return at(z, ring_y(d), x, c)

    def on_z(d):
        return at(ring_z(d), y, x, c)

    def on_x(d):
        return at(z, y, ring_x(d), c)

    partner = at(z, y, x, 1 - c)
    mirror = at(NZ - 1 - z, y, x, c)
    swap_to = (at(z, ring_y(1), x, 1 - c), at(z, ring_y(-1), x, 1 - c))
    barrier = pltpu.get_barrier_semaphore()
    greet(barrier, [on_y(d) for d in range(1, NY)])
    greet(barrier, [on_z(d) for d in range(1, NZ)])
    greet(barrier, [on_x(d) for d in range(1, NX)])
    greet(barrier, [at(z, y, ring_x(d), 1 - c) for d in range(NX)])
    greet(barrier, swap_to)
    sends = []
    guarded = []

    def launch(copy):
        copy.start()
        sends.append(copy)

    def launch_if(condition, make):
        @pl.when(condition)
        def _():
            make().start()

        guarded.append((condition, make))

    experts = ((r.gate_hbm, r.gate), (r.up_hbm, r.up), (r.down_hbm, r.down))
    own_rows = pl.ds(0, HIDDEN)
    piece_rows = (pl.ds(HIDDEN, PIECE), pl.ds(HIDDEN + PIECE, PIECE))

    def load(m):
        hbm, ref = experts[m]
        return pltpu.make_async_copy(hbm, ref.at[own_rows], r.load_sem.at[m])

    @pl.when(keeper)
    def _():
        for m in range(3):
            load(m).start()

    rates = r.rates[...]
    length = r.query.shape[0]
    gap = (
        lax.broadcasted_iota(jnp.int32, (length, length), 0)
        - lax.broadcasted_iota(jnp.int32, (length, length), 1)
    ).astype(F32)
    position = lax.broadcasted_iota(jnp.int32, (length, 1), 0).astype(F32)

    def head(ref, h):
        return ref[:, 128 * h : 128 * (h + 1)]

    for h in range(4):
        fade = jnp.exp(-rates[:, h : h + 1] * (length - 1.0 - position))
        faded = (head(r.key, h).astype(F32) * fade).astype(BF16)
        r.local_out[h] = tn_dot(faded, head(r.value, h)).astype(BF16)
    r.proj[z] = r.weight[...]
    pl.semaphore_wait(barrier, NY - 1 + NZ - 1 + NX - 1 + NX + 2)

    for d in (2, 1, 3):
        launch(
            remote(
                r.local_out.at[ring_y(d)], r.local_in.at[y], r.local_s.at[d], r.local_r.at[d], on_y(d)
            )
        )
    r.local_in[y] = r.local_out[y]

    def z_parts(k):
        if k < 4:
            return r.proj.at[ring_z(1 - k)], r.proj.at[ring_z(k - 1)]
        return r.proj.at[ring_z(-3)].at[pl.ds(0, 48)], r.proj.at[ring_z(3)].at[pl.ds(48, 48)]

    def z_step(k):
        a, b = z_parts(k)
        launch(remote(a, a, r.proj_s.at[0, k], r.proj_r.at[0, k], on_z(1)))
        launch(remote(b, b, r.proj_s.at[1, k], r.proj_r.at[1, k], on_z(-1)))

    def z_wait(k):
        if k < 4:
            a, b = r.proj.at[ring_z(-k)], r.proj.at[ring_z(k)]
        else:
            a, b = r.proj.at[ring_z(4)].at[pl.ds(0, 48)], r.proj.at[ring_z(4)].at[pl.ds(48, 48)]
        await_copy(a, r.proj_s.at[0, k], r.proj_r.at[0, k], on_z(1))
        await_copy(b, r.proj_s.at[1, k], r.proj_r.at[1, k], on_z(-1))

    z_step(1)
    for m in range(3):
        launch_if(
            keeper,
            lambda m=m: remote(
                experts[m][0], experts[m][1].at[own_rows], r.own_s.at[m], r.own_r.at[m], partner
            ),
        )

    for h in range(4):
        decay = jnp.where(gap >= 0, jnp.exp(-rates[:, h : h + 1] * jnp.maximum(gap, 0.0)), 0.0)
        scores = nt_dot(head(r.query, h), head(r.key, h))
        r.intra[h] = dot((scores * decay).astype(BF16), head(r.value, h))

    for d in (1, 3, 2):
        await_copy(r.local_in.at[ring_y(-d)], r.local_s.at[d], r.local_r.at[d], on_y(d))
    lane = lax.broadcasted_iota(jnp.int32, rates.shape, 1)
    own_rate = jnp.sum(jnp.where(lane == y, rates, 0.0), axis=1, keepdims=True)

    def power(n):
        return jnp.exp(-own_rate * (128.0 * n))

    locals_in = [r.local_in[i].astype(F32) for i in range(NY)]
    total = locals_in[3]
    for i in range(3):
        total = total + power(3 - i) * locals_in[i]
    r.total_out[...] = total.astype(BF16)
    for d in range(NZ - 1, 0, -1):
        launch_if(
            z + d < NZ,
            lambda d=d: remote(
                r.total_out, r.total_in.at[z], r.total_s.at[d], r.total_r.at[d], on_z(d)
            ),
        )
    z_wait(1)
    z_step(2)
    r.entry[...] = jnp.zeros_like(r.entry)
    for d in range(1, NZ):

        @pl.when(z >= d)
        def _(d=d):
            await_copy(r.total_in.at[ring_z(-d)], r.total_s.at[d], r.total_r.at[d], on_z(d))
            r.entry[...] += power(4 * (d - 1)) * r.total_in[ring_z(-d)].astype(F32)

    incoming = r.entry[...]
    for i in range(NY):
        r.state_out[i] = incoming.astype(BF16)
        incoming = power(1) * incoming + locals_in[i]
    for d in (2, 1, 3):
        launch(
            remote(
                r.state_out.at[ring_y(d)], r.state_in.at[y], r.state_s.at[d], r.state_r.at[d], on_y(d)
            )
        )
    r.state_in[y] = r.state_out[y]
    z_wait(2)
    z_step(3)
    for d in (1, 3, 2):
        await_copy(r.state_in.at[ring_y(-d)], r.state_s.at[d], r.state_r.at[d], on_y(d))
    for h in range(4):
        fade = jnp.exp(-rates[:, h : h + 1] * (position + 1.0))
        mixed = r.intra[h] + fade * dot(head(r.query, h), r.state_in[h])
        mean = jnp.mean(mixed * mixed, axis=-1, keepdims=True)
        out = (mixed * lax.rsqrt(mean + EPSILON)).astype(BF16)
        for e in range(8):
            r.heads[y, e // 2, e % 2, :, 128 * h : 128 * (h + 1)] = out[16 * e : 16 * (e + 1)]
    for d in (2, 1, 3):
        launch(remote(r.heads.at[y], r.heads.at[y], r.heads_s.at[d], r.heads_r.at[d], on_y(d)))
    z_wait(3)
    z_step(4)

    for m in range(3):
        for side in range(2):
            launch_if(
                jnp.logical_not(keeper),
                lambda m=m, side=side: remote(
                    experts[m][0].at[pl.ds(side * PIECE, PIECE)],
                    experts[m][1].at[piece_rows[side]],
                    r.swap_s.at[m, side],
                    r.swap_r.at[m, side],
                    swap_to[side],
                ),
            )

    def pass_on(m):
        for side in range(2):
            ref = experts[m][1].at[piece_rows[side]]

            @pl.when(jnp.logical_not(keeper))
            def _(m=m, side=side, ref=ref):
                await_copy(ref, r.swap_s.at[m, side], r.swap_r.at[m, side], swap_to[1 - side])

            launch_if(
                jnp.logical_not(keeper),
                lambda m=m, side=side, ref=ref: remote(
                    ref, ref, r.pass_s.at[m, side], r.pass_r.at[m, side], partner
                ),
            )

    def weights_ready():
        @pl.when(keeper)
        def _():
            for m in range(3):
                load(m).wait()
                for side in range(2):
                    ref = experts[m][1].at[piece_rows[side]]
                    await_copy(ref, r.pass_s.at[m, side], r.pass_r.at[m, side], partner)

        @pl.when(jnp.logical_not(keeper))
        def _():
            for m in range(3):
                ref = experts[m][1].at[own_rows]
                await_copy(ref, r.own_s.at[m], r.own_r.at[m], partner)

    for d in (1, 3, 2):
        await_copy(r.heads.at[ring_y(-d)], r.heads_s.at[d], r.heads_r.at[d], on_y(d))
    z_wait(4)

    def project(which):
        lhs = r.heads[:, :, which].reshape(256, 512)
        return nt_dot(lhs, r.proj[...].reshape(768, 512)).reshape(4, 4, 16, 768)

    r.pair_out[...] = project(1 - c).astype(BF16)
    pair_copy = remote(r.pair_out, r.pair_in, r.pair_s.at[0], r.pair_r.at[0], partner)
    launch(pair_copy)
    r.part[...] = project(c)
    pair_copy.wait_recv()
    r.part[...] += r.pair_in[...].astype(F32)
    r.part_out[...] = r.part[...].astype(BF16)
    for d in (2, 1, 3):
        launch(
            remote(
                r.part_out.at[:, ring_x(d)], r.part_in.at[x], r.part_s.at[d], r.part_r.at[d], on_x(d)
            )
        )
    slab = r.part[:, x]
    for d in (1, 3, 2):
        await_copy(r.part_in.at[ring_x(-d)], r.part_s.at[d], r.part_r.at[d], on_x(d))
        slab = slab + r.part_in[ring_x(-d)].astype(F32)
    r.slab[...] = slab
    r.slab_out[...] = slab.astype(BF16)
    for d in (2, 1, 3):
        launch(
            remote(
                r.slab_out.at[ring_y(d)], r.slab_in.at[y], r.slab_s.at[d], r.slab_r.at[d], on_y(d)
            )
        )
    for d in (1, 3, 2):
        await_copy(r.slab_in.at[ring_y(-d)], r.slab_s.at[d], r.slab_r.at[d], on_y(d))
        r.slab[ring_y(-d)] = r.slab_in[ring_y(-d)].astype(F32)
    attended = jnp.concatenate(
        [r.slab[yy][:, SHARD * zz : SHARD * (zz + 1)] for zz in range(NZ) for yy in range(NY)], axis=1
    )
    hidden = r.stream[...].astype(F32) + attended
    r.hidden[...] = hidden
    mean = jnp.mean(hidden * hidden, axis=-1, keepdims=True)
    r.tokens[x, c] = (hidden * lax.rsqrt(mean + EPSILON) * r.gain[...]).astype(BF16)
    square = lax.broadcasted_iota(jnp.int32, (16, 16), 0) == lax.broadcasted_iota(
        jnp.int32, (16, 16), 1
    )

    def upright(row):
        wide = jnp.where(square, jnp.broadcast_to(row, (16, 16)).astype(F32), 0.0)
        return jnp.sum(wide, axis=1, keepdims=True)

    table_lane = lax.broadcasted_iota(jnp.int32, (16, 128), 1)
    r.tables[x, c] = jnp.where(
        table_lane == 0, upright(r.routes[0:1, :]), upright(r.routes[1:2, :])
    ).astype(jnp.int32)

    for d in (2, 1, 3, 0):
        for n, ref in enumerate((r.tokens, r.tables)):

            def make(d=d, n=n, ref=ref):
                block = ref.at[x, c]
                device = at(z, y, ring_x(d), core)
                return remote(block, block, r.tok_s.at[n, d], r.tok_r.at[n, d, c], device)

            if d:
                launch(make())
            else:
                launch_if(jnp.logical_not(source), make)

    pass_on(0)
    pass_on(1)

    low_lane = lax.broadcasted_iota(jnp.int32, (128, CHUNK), 1) < SLOTS

    def expert_of(rel, t):
        return x * 4 + t * 2 + (half if rel == 0 else 1 - half)

    @pl.when(source)
    def _():
        for d in (0, 1, 3, 2):
            for n, ref in enumerate((r.tokens, r.tables)):
                for other in range(2):
                    if d == 0 and other == 1:
                        continue
                    cc = 1 - c if d == 0 else other
                    block = ref.at[ring_x(-d), cc]
                    await_copy(block, r.tok_s.at[n, d], r.tok_r.at[n, d, cc], on_x(d))
        rows = r.tokens[...].reshape(128, DM)
        table = r.tables[...].reshape(128, 128)
        first, second = table[:, 0:1], table[:, 1:2]
        lanes = lax.broadcasted_iota(jnp.int32, (128, 128), 1)
        earlier = (lanes < lax.broadcasted_iota(jnp.int32, (128, 128), 0)).astype(BF16)
        for rel in (1, 0):
            for t in range(2):
                expert = expert_of(rel, t)
                hit = jnp.logical_or(first == expert, second == expert)
                wide = jnp.broadcast_to(jnp.where(hit, 1.0, 0.0), (128, 128))
                rank = dot(earlier, wide.astype(BF16)).astype(jnp.int32)
                low = jnp.where(rank == lanes, wide, 0.0)[:, :CHUNK]
                high = jnp.where(rank == lanes - SLOTS, wide, 0.0)[:, :CHUNK]
                low = jnp.where(low_lane, low, 0.0).astype(BF16)
                high = jnp.where(low_lane, 0.0, high).astype(BF16)
                r.sel[rel, t, 0] = low
                r.sel[rel, t, 1] = high
                chunk = (tn_dot(low, rows[:, :HALF]) + tn_dot(high, rows[:, HALF:])).astype(BF16)
                if rel == 0:
                    r.line[t, zl] = chunk
                else:
                    r.cross[t] = chunk
                    remote(
                        r.cross.at[t], r.line.at[t, 3 - zl], r.cross_s.at[t], r.cross_r.at[t], mirror
                    ).start()

    @pl.when(jnp.logical_not(source))
    def _():
        for t in range(2):
            await_copy(r.line.at[t, zl], r.cross_s.at[t], r.cross_r.at[t], mirror)

    order = [zl, zl + 1 - 2 * (zl % 2), 2 - zl // 2, 3 - 3 * (zl // 2)]

    def spread(i):
        p = order[i]
        for t in range(2):
            s = r.line.at[t, p]
            if i > 0:
                await_copy(s, r.line_s.at[0, t, p], r.line_r.at[t, p], on_z(1))
            launch_if(
                jnp.logical_and(p <= zl, zl < 3),
                lambda s=s, t=t, p=p: remote(
                    s, s, r.line_s.at[0, t, p], r.line_r.at[t, p], on_z(1)
                ),
            )
            launch_if(
                jnp.logical_and(p >= zl, zl > 0),
                lambda s=s, t=t, p=p: remote(
                    s, s, r.line_s.at[1, t, p], r.line_r.at[t, p], on_z(-1)
                ),
            )
        for j, d, t in ((0, 2, role), (1, 1, 1 - role), (2, -1, 1 - role)):
            launch(
                remote(
                    r.line.at[t, p], r.got.at[j, p], r.got_s.at[j, p], r.got_r.at[j, p], on_y(d)
                )
            )

    for i in range(4):
        spread(i)

    pass_on(2)

    @pl.when(source)
    def _():
        logits = nt_dot(r.tokens[...].reshape(128, DM), r.router[...])
        table = r.tables[...].reshape(128, 128)
        first, second = table[:, 0:1], table[:, 1:2]
        expert = lax.broadcasted_iota(jnp.int32, logits.shape, 1)

        def lifted(chosen):
            logit = jnp.sum(jnp.where(expert == chosen, logits, 0.0), axis=1, keepdims=True)
            return jax.nn.sigmoid(logit)

        lift_first, lift_second = lifted(first), lifted(second)
        both = lift_first + lift_second
        for rel in range(2):
            for t in range(2):
                chosen = expert_of(rel, t)
                share = jnp.where(first == chosen, lift_first / both, 0.0) + jnp.where(
                    second == chosen, lift_second / both, 0.0
                )
                r.share[rel, t] = jnp.broadcast_to(share, (128, 128))

    def arrived(i):
        p = order[i]
        for j, d in ((0, 2), (1, 1), (2, -1)):
            await_copy(r.got.at[j, p], r.got_s.at[j, p], r.got_r.at[j, p], on_y(d))

    def compute(which):
        chunks = []
        for i in which:
            p = order[i]
            chunks += [r.line[role, p]] + [r.got[j, p] for j in range(3)]
        for n in range(4):
            a, b = chunks[2 * n].astype(F32), chunks[2 * n + 1].astype(F32)
            rows = slice(CHUNK * n, CHUNK * (n + 1))
            r.flat[rows, :HALF] = jnp.concatenate([a[:SLOTS], b[:SLOTS]], axis=0).astype(BF16)
            r.flat[rows, HALF:] = jnp.concatenate([a[SLOTS:], b[SLOTS:]], axis=0).astype(BF16)
        rows = r.flat[...]
        gated = nt_dot(rows, r.gate[...])
        inner = (gated * jax.nn.sigmoid(gated) * nt_dot(rows, r.up[...])).astype(BF16)
        left = dot(inner, r.down[:, :HALF])
        right = dot(inner, r.down[:, HALF:])
        for n, i in enumerate(which):
            for j in range(4):
                rows = slice(SLOTS * (4 * n + j), SLOTS * (4 * n + j + 1))
                r.partial[j, order[i]] = jnp.concatenate([left[rows], right[rows]], axis=0).astype(BF16)

    def give_back(i):
        p = order[i]
        for j, d in ((0, 2), (1, -1), (2, 1)):
            launch(
                remote(
                    r.partial.at[j + 1, p], r.back.at[j, p], r.back_s.at[j, p], r.back_r.at[j, p], on_y(d)
                )
            )

    arrived(0)
    arrived(1)
    weights_ready()
    compute((0, 1))
    arrived(2)
    arrived(3)
    compute((3, 2))
    for i in (3, 2, 1, 0):
        give_back(i)

    def collect(i):
        p = order[i]
        for j, d in ((0, 2), (1, 1), (2, -1)):
            await_copy(r.back.at[j, p], r.back_s.at[j, p], r.back_r.at[j, p], on_y(d))
        r.total[role, p] = r.partial[0, p].astype(F32) + r.back[0, p].astype(F32)
        r.total[1 - role, p] = r.back[1, p].astype(F32) + r.back[2, p].astype(F32)

    def add_line(t, p, side):
        await_copy(r.line_in.at[side, t, p], r.sum_s.at[t, p], r.sum_r.at[side, t, p], on_z(1))
        r.total[t, p] += r.line_in[side, t, p].astype(F32)

    def along(i):
        p = order[i]
        for t in range(2):

            @pl.when(jnp.logical_and(p > zl, zl > 0))
            def _(t=t):
                add_line(t, p, 0)

            @pl.when(jnp.logical_and(p < zl, zl < 3))
            def _(t=t):
                add_line(t, p, 1)

            r.line_out[t, p] = r.total[t, p].astype(BF16)
            for side, condition in ((0, p > zl), (1, p < zl)):
                launch_if(
                    condition,
                    lambda t=t, p=p, side=side: remote(
                        r.line_out.at[t, p],
                        r.line_in.at[side, t, p],
                        r.sum_s.at[t, p],
                        r.sum_r.at[side, t, p],
                        on_z(-1 if side else 1),
                    ),
                )

    for i in (3, 2, 1):
        collect(i)
        along(i)
    collect(0)
    for t in range(2):

        @pl.when(zl > 0)
        def _(t=t):
            add_line(t, zl, 0)

        @pl.when(zl < 3)
        def _(t=t):
            add_line(t, zl, 1)

        r.final[t] = r.total[t, zl].astype(BF16)
        launch_if(
            jnp.logical_not(source),
            lambda t=t: remote(r.final.at[t], r.ret.at[t], r.ret_s.at[t], r.ret_r.at[t], mirror),
        )

    @pl.when(source)
    def _():
        for rel in range(2):
            for t in range(2):
                if rel == 1:
                    await_copy(r.ret.at[t], r.ret_s.at[t], r.ret_r.at[t], mirror)
                rows = (r.ret if rel else r.final)[t]
                share = r.share[rel, t][:, 0:1]
                for side in range(2):
                    cols = slice(HALF * side, HALF * (side + 1))
                    value = (share * dot(r.sel[rel, t, side], rows)).reshape(4, 2, 16, HALF)
                    if rel == 0 and t == 0:
                        r.mixed[:, :, :, cols] = value
                    else:
                        r.mixed[:, :, :, cols] += value
        r.home_out[...] = r.mixed[...].astype(BF16)
        r.home[...] = r.mixed[x, c]

    for d in (2, 1, 3, 0):
        for other in range(2):
            if d == 0 and other == 1:
                continue
            cc = 1 - c if d == 0 else other
            launch_if(
                source,
                lambda d=d, cc=cc: remote(
                    r.home_out.at[ring_x(d), cc],
                    r.home_in.at[x],
                    r.home_s.at[d, cc],
                    r.home_r.at[d],
                    at(z, y, ring_x(d), cc),
                ),
            )

    @pl.when(jnp.logical_not(source))
    def _():
        await_copy(r.home_in.at[x], r.home_s.at[0, c], r.home_r.at[0], partner)
        r.home[...] = r.home_in[x].astype(F32)

    result = r.hidden[...] + r.home[...]
    for d in (1, 3, 2):
        await_copy(r.home_in.at[ring_x(-d)], r.home_s.at[d, c], r.home_r.at[d], on_x(d))
        result = result + r.home_in[ring_x(-d)].astype(F32)
    r.out[...] = result.astype(BF16)

    @pl.when(source)
    def _():
        for t in range(2):
            remote(
                r.cross.at[t], r.line.at[t, 3 - zl], r.cross_s.at[t], r.cross_r.at[t], mirror
            ).wait_send()

    for condition, make in guarded:

        @pl.when(condition)
        def _(make=make):
            make().wait_send()

    for copy in sends:
        copy.wait_send()


VMEM = pl.BlockSpec(memory_space=pltpu.VMEM)
ANY = pl.BlockSpec(memory_space=pl.ANY)


def body(
    stream,
    query,
    key,
    value,
    decay_rate,
    out_weight,
    norm_gain,
    router_weight,
    routes,
    expert_gate,
    expert_up,
    expert_down,
):
    return pl.pallas_call(
        kernel,
        out_shape=jax.ShapeDtypeStruct(stream.shape, BF16),
        in_specs=[VMEM] * 9 + [ANY] * 3,
        out_specs=VMEM,
        scratch_shapes=list(SCRATCH.values()),
        compiler_params=pltpu.CompilerParams(
            collective_id=0, has_side_effects=True, vmem_limit_bytes=56 * 2**20
        ),
        name="whole",
    )(
        stream,
        query,
        key,
        value,
        decay_rate.reshape(1, 4),
        out_weight.T,
        norm_gain.reshape(1, DM),
        routes.T,
        router_weight.T,
        expert_gate.T,
        expert_up.T,
        expert_down,
    )


def solution(mesh):
    placed = (
        P(("ctx", "ep"), None),
        P("ctx", "ep"),
        P("ctx", "ep"),
        P("ctx", "ep"),
        P("ep"),
        P("ep", "ctx"),
        P(),
        P(),
        P(("ctx", "ep"), None),
        P(None, ("ep", "ctx")),
        P(None, ("ep", "ctx")),
        P(("ep", "ctx"), None),
    )
    return jax.shard_map(
        body, mesh=mesh, in_specs=placed, out_specs=P(("ctx", "ep"), None), check_vma=False
    )
```

time: 761 us -> 157 us (0.21)
  waiting for transfers between devices: 345 us -> 0 us
  starting transfers between devices: 195 us -> 0 us
  Pallas kernels: 0 us -> 155 us
  blocking collectives: 128 us -> 0 us
  local copies, waits for them, and re-layouts: 43.6 us -> 1.54 us
  matrix products: 23.5 us -> 0 us
  between operations: 13.6 us -> 0.01 us
  other arithmetic: 9.81 us -> 0 us
    ppermute x31 -> x0, starting transfers between devices: 182 us -> none  [shifted(): return lax.ppermute(shard, axis, pairs)]
    pallas_call x0 -> x1, Pallas kernels: none -> 155 us  [body(): pl.pallas_call(kernel, out_shape=jax.ShapeDtypeStruct(stream.shape, BF16)...]
    ppermute x31 -> x0, waiting for transfers between devices: 129 us -> none  [shifted(): return lax.ppermute(shard, axis, pairs)]
    all_to_all x2 -> x0, blocking collectives: 128 us -> none  [the longest x1 115 us: body(): lax.all_to_all(fanned, 'ctx', split_axis=0, concat_axis=0, tiled=True)]
    all_to_all x2 -> x0, waiting for transfers between devices: 109 us -> none  [the longest x1 102 us: body(): lax.all_to_all(partial_out.astype(jnp.bfloat16), 'ctx', split_axis=0, con...]
    reduce_scatter x1 -> x0, waiting for transfers between devices: 106 us -> none  [body(): lax.psum_scatter(partial_value.astype(jnp.bfloat16), 'ep', scatter_dimens...]
    dot_general x9 -> x0, matrix products: 23.5 us -> none  [the longest x1 10.4 us: body(): jnp.dot(inner_act, expert_down, preferred_element_type=jnp.float32)]
    convert_element_type x3 -> x0, local copies, waits for them, and re-layouts: 20 us -> none  [the longest x2 19 us: body(): partial_out.astype(jnp.bfloat16)]
  transfers between devices with their start and end apart: 35 -> 0, of which waited for: 34 -> 0; matrix products, arithmetic and copies ran while one was open for 1% -> 0% of each run, Pallas kernels for 0% -> 0%
where the time goes in v2:
time: 157 us
  Pallas kernels  155 us (99%)
    pallas_call x1, Pallas kernels, body(): pl.pallas_call(kernel, out_shape=jax.ShapeDtypeStruct(stream.shape, BF16)...  155 us

profile of v2, /device:TPU:1, one launch (start us, length us, event | category | flops | bytes accessed | tf_op | source)
XLA Modules:
  0.0 156.9 jit_solution(8081948273166412799)
XLA Ops:
  0.0 155.3 %whole.1 = bf16[16,3072]{1,0:T(8,128)(2,1)} custom-call(bf16[16,3072]{1,0:T(8,128)(2,1)} %refs_0_.1, bf16[128,512]{1,0:T(8,128)(2,1)} %refs_1_.1, bf16[128,512]{1,0:T(8,128)(2,1)} %refs_2_.1, bf16[128,512]{1,0:T(8,128)(2,1)} %refs_3_.1, f32[1,4]{1,0:T(1,128)} %bitcast.13, bf16[96,512]{1,0:T(8,128)(2,1)} %bitcast.9, f32[1,3072]{1,0:T(1,128)} %bitcast.11, ...), custom_call_target="tpu_custom_call" | custom-call | tf_op jit(solution)/shard_map/whole/pallas_call | solution.py:721
  155.4 1.5 copy.14

commit v3 on v2

v3 whole, which is shorter than its diff:
```python
import jax
import jax.numpy as jnp
from jax import lax
from jax.experimental import pallas as pl
from jax.experimental.pallas import tpu as pltpu
from jax.sharding import PartitionSpec as P

EPSILON = 1e-06
MESH = pl.DeviceIdType.MESH
F32 = jnp.float32
BF16 = jnp.bfloat16
NY = 4
NZ = 8
NX = 4
DM = 3072
HALF = 1536
SLOTS = 24
CHUNK = 48
SHARD = 96
HIDDEN = 288
PIECE = 96
PART = 48


def bf(*shape):
    return pltpu.VMEM(shape, BF16)


def fl(*shape):
    return pltpu.VMEM(shape, F32)


def dma(*shape):
    return pltpu.SemaphoreType.DMA(shape)


INPUTS = (
    "stream", "query", "key", "value", "rates", "weight", "gain", "routes", "router",
    "gate_hbm", "up_hbm", "down_hbm", "out",
)
SCRATCH = dict(
    intra=fl(4, 128, 128),
    key_in=bf(4, 128, 128),
    value_in=bf(4, 128, 128),
    query_in=bf(4, 128, 128),
    local=fl(4, 128, 128),
    total_out=bf(128, 128),
    total_in=bf(8, 128, 128),
    entry=fl(128, 128),
    proj=bf(8, SHARD, 512),
    heads=bf(4, 4, 4, 2, 16, 128),
    pair_out=bf(2, 4, 4, 16, 384),
    pair_in=bf(2, 4, 4, 16, 384),
    part=fl(2, 4, 4, 16, 384),
    part_out=bf(2, 4, 4, 16, 384),
    part_in=bf(2, 4, 4, 16, 384),
    slab=fl(2, 4, 16, 384),
    slab_out=bf(2, 4, 16, 384),
    slab_in=bf(2, 4, 16, 384),
    hidden=fl(16, DM),
    tokens=bf(4, 2, 16, DM),
    tables=pltpu.VMEM((4, 2, 16, 128), jnp.int32),
    gate=bf(2 * HIDDEN, DM),
    up=bf(2 * HIDDEN, DM),
    down=bf(2 * HIDDEN, DM),
    sel=bf(2, 2, 2, 128, CHUNK),
    share=fl(2, 2, 128, 128),
    cross=bf(2, CHUNK, HALF),
    line=bf(2, 4, CHUNK, HALF),
    got=bf(3, 4, CHUNK, HALF),
    flat=bf(192, DM),
    partial=bf(4, 4, CHUNK, HALF),
    back=bf(3, 4, CHUNK, HALF),
    total=fl(2, 4, CHUNK, HALF),
    line_out=bf(2, 4, CHUNK, HALF),
    line_in=bf(2, 2, 4, CHUNK, HALF),
    ret=bf(2, CHUNK, HALF),
    mixed=fl(4, 2, 16, DM),
    home_out=bf(4, 2, 16, DM),
    home_in=bf(4, 16, DM),
    home=fl(16, DM),
    load_sem=dma(3),
    block_s=dma(3, 4), block_r=dma(3, 4),
    total_s=dma(8), total_r=dma(8),
    proj_s=dma(2, 5), proj_r=dma(2, 5),
    heads_s=dma(4), heads_r=dma(4),
    pair_s=dma(2), pair_r=dma(2),
    part_s=dma(2, 4), part_r=dma(2, 4),
    slab_s=dma(2, 4), slab_r=dma(2, 4),
    tok_s=dma(2, 4), tok_r=dma(2, 4, 2),
    own_s=dma(3), own_r=dma(3),
    swap_s=dma(3, 2, 3), swap_r=dma(3, 2, 3),
    pass_s=dma(3, 2, 3), pass_r=dma(3, 2, 3),
    cross_s=dma(2, 2),
    line_s=dma(2, 2, 4, 2), line_r=dma(2, 4, 2),
    got_s=dma(3, 4), got_r=dma(3, 4),
    back_s=dma(3, 4), back_r=dma(3, 4),
    sum_s=dma(2, 4, 2), sum_r=dma(2, 2, 4, 2),
    ret_r=dma(2, 2),
    home_s=dma(2, 4, 2), home_r=dma(2, 4),
)


class Refs:
    def __init__(self, refs):
        for name, ref in zip(INPUTS + tuple(SCRATCH), refs, strict=True):
            setattr(self, name, ref)


def at(z, y, x, c):
    return (z * NY + y, x * 2 + c)


def remote(src, dst, send, recv, device):
    return pltpu.make_async_remote_copy(
        src_ref=src,
        dst_ref=dst,
        send_sem=send,
        recv_sem=recv,
        device_id=device,
        device_id_type=MESH,
    )


def await_copy(dst, send, recv, device):
    remote(dst, dst, send, recv, device).wait_recv()


def greet(barrier, devices):
    for device in devices:
        pl.semaphore_signal(barrier, inc=1, device_id=device, device_id_type=MESH)


def nt_dot(a, b):
    return lax.dot_general(a, b, (((1,), (1,)), ((), ())), preferred_element_type=F32)


def tn_dot(a, b):
    return lax.dot_general(a, b, (((0,), (0,)), ((), ())), preferred_element_type=F32)


def dot(a, b):
    return jnp.dot(a, b, preferred_element_type=F32)


def kernel(*refs):
    r = Refs(refs)
    ctx = lax.axis_index("ctx")
    ep = lax.axis_index("ep")
    z, y, x, c = ctx // NY, ctx % NY, ep // 2, ep % 2
    half, zl = z // 4, z % 4
    role = (y + z) % 2
    source = z % 2 == c
    keeper = c == role
    core = z % 2

    def ring_y(d):
        return lax.rem(y + d + NY, NY)

    def ring_z(d):
        return lax.rem(z + d + NZ, NZ)

    def ring_x(d):
        return lax.rem(x + d + NX, NX)

    def on_y(d):
        return at(z, ring_y(d), x, c)

    def on_z(d):
        return at(ring_z(d), y, x, c)

    def on_x(d):
        return at(z, y, ring_x(d), c)

    partner = at(z, y, x, 1 - c)
    beside = z + 1 - 2 * (z % 2)
    swap_to = (
        at(z, ring_y(1), x, 1 - c),
        at(z, ring_y(-1), x, 1 - c),
        at(beside, y, x, 1 - c),
    )
    barrier = pltpu.get_barrier_semaphore()
    greet(barrier, [on_y(d) for d in range(1, NY)])
    greet(barrier, [on_z(d) for d in range(1, NZ)])
    greet(barrier, [on_x(d) for d in range(1, NX)])
    greet(barrier, [at(z, y, ring_x(d), 1 - c) for d in range(NX)])
    greet(barrier, swap_to)
    sends = []
    guarded = []

    def launch(copy):
        copy.start()
        sends.append(copy)

    def launch_if(condition, make):
        @pl.when(condition)
        def _():
            make().start()

        guarded.append((condition, make))

    experts = ((r.gate_hbm, r.gate), (r.up_hbm, r.up), (r.down_hbm, r.down))
    own_rows = pl.ds(0, HIDDEN)

    def part_rows(base, k, side):
        return pl.ds(base + side * PIECE + k * PART, PART)

    def load(m):
        hbm, ref = experts[m]
        return pltpu.make_async_copy(hbm, ref.at[own_rows], r.load_sem.at[m])

    @pl.when(keeper)
    def _():
        for m in range(3):
            load(m).start()

    away = jnp.logical_not(keeper)
    back_side = (1, 0, 2)

    def swap(sides, units):
        for unit in units:
            m, k = divmod(unit, 2)
            for side in sides:
                launch_if(
                    away,
                    lambda m=m, k=k, side=side: remote(
                        experts[m][0].at[part_rows(0, k, side)],
                        experts[m][1].at[part_rows(HIDDEN, k, side)],
                        r.swap_s.at[m, k, side],
                        r.swap_r.at[m, k, side],
                        swap_to[side],
                    ),
                )

    def pass_on(sides, units):
        for unit in units:
            m, k = divmod(unit, 2)
            for side in sides:
                ref = experts[m][1].at[part_rows(HIDDEN, k, side)]

                @pl.when(away)
                def _(m=m, k=k, side=side, ref=ref):
                    await_copy(
                        ref,
                        r.swap_s.at[m, k, side],
                        r.swap_r.at[m, k, side],
                        swap_to[back_side[side]],
                    )

                launch_if(
                    away,
                    lambda m=m, k=k, side=side, ref=ref: remote(
                        ref, ref, r.pass_s.at[m, k, side], r.pass_r.at[m, k, side], partner
                    ),
                )

    def weights_ready():
        @pl.when(keeper)
        def _():
            for m in range(3):
                load(m).wait()
                for k in range(2):
                    for side in range(3):
                        ref = experts[m][1].at[part_rows(HIDDEN, k, side)]
                        await_copy(ref, r.pass_s.at[m, k, side], r.pass_r.at[m, k, side], partner)

        @pl.when(away)
        def _():
            for m in range(3):
                ref = experts[m][1].at[own_rows]
                await_copy(ref, r.own_s.at[m], r.own_r.at[m], partner)

    rates = r.rates[...]
    length = r.query.shape[0]
    gap = (
        lax.broadcasted_iota(jnp.int32, (length, length), 0)
        - lax.broadcasted_iota(jnp.int32, (length, length), 1)
    ).astype(F32)
    position = lax.broadcasted_iota(jnp.int32, (length, 1), 0).astype(F32)
    lane = lax.broadcasted_iota(jnp.int32, rates.shape, 1)
    own_rate = jnp.sum(jnp.where(lane == y, rates, 0.0), axis=1, keepdims=True)

    def power(n):
        return jnp.exp(-own_rate * (128.0 * n))

    def head_columns(h):
        return pl.ds(pl.multiple_of(h * 128, 128), 128)

    blocks = ((r.key, r.key_in), (r.value, r.value_in), (r.query, r.query_in))
    for whole, own in blocks:
        own[y] = whole[:, head_columns(y)]
    r.proj[z] = r.weight[...]
    pl.semaphore_wait(barrier, NY - 1 + NZ - 1 + NX - 1 + NX + 3)

    for n, (whole, own) in enumerate(blocks):
        for d in (2, 1, 3):
            launch(
                remote(
                    whole.at[:, head_columns(ring_y(d))],
                    own.at[y],
                    r.block_s.at[n, d],
                    r.block_r.at[n, d],
                    on_y(d),
                )
            )

    def block_wait(n, d):
        await_copy(blocks[n][1].at[ring_y(-d)], r.block_s.at[n, d], r.block_r.at[n, d], on_y(d))

    def z_parts(k):
        if k < 4:
            return r.proj.at[ring_z(1 - k)], r.proj.at[ring_z(k - 1)]
        return r.proj.at[ring_z(-3)].at[pl.ds(0, 48)], r.proj.at[ring_z(3)].at[pl.ds(48, 48)]

    def z_step(k):
        a, b = z_parts(k)
        launch(remote(a, a, r.proj_s.at[0, k], r.proj_r.at[0, k], on_z(1)))
        launch(remote(b, b, r.proj_s.at[1, k], r.proj_r.at[1, k], on_z(-1)))

    def z_wait(k):
        if k < 4:
            a, b = r.proj.at[ring_z(-k)], r.proj.at[ring_z(k)]
        else:
            a, b = r.proj.at[ring_z(4)].at[pl.ds(0, 48)], r.proj.at[ring_z(4)].at[pl.ds(48, 48)]
        await_copy(a, r.proj_s.at[0, k], r.proj_r.at[0, k], on_z(1))
        await_copy(b, r.proj_s.at[1, k], r.proj_r.at[1, k], on_z(-1))

    z_step(1)
    swap((0, 1), (0,))
    for m in range(3):
        launch_if(
            keeper,
            lambda m=m: remote(
                experts[m][0], experts[m][1].at[own_rows], r.own_s.at[m], r.own_r.at[m], partner
            ),
        )

    fade = jnp.exp(-own_rate * (length - 1.0 - position))
    for d in (0, 1, 3, 2):
        if d:
            block_wait(0, d)
            block_wait(1, d)
        i = ring_y(-d)
        faded = (r.key_in[i].astype(F32) * fade).astype(BF16)
        r.local[i] = tn_dot(faded, r.value_in[i])
    swap((0, 1), (1,))
    total = r.local[3]
    for i in range(3):
        total = total + power(3 - i) * r.local[i]
    r.total_out[...] = total.astype(BF16)
    for d in range(NZ - 1, 0, -1):
        launch_if(
            z + d < NZ,
            lambda d=d: remote(
                r.total_out, r.total_in.at[z], r.total_s.at[d], r.total_r.at[d], on_z(d)
            ),
        )
    z_wait(1)
    z_step(2)
    decay = jnp.where(gap >= 0, jnp.exp(-own_rate * jnp.maximum(gap, 0.0)), 0.0)
    for d in (0, 1, 3, 2):
        if d:
            block_wait(2, d)
        i = ring_y(-d)
        scores = nt_dot(r.query_in[i], r.key_in[i])
        r.intra[i] = dot((scores * decay).astype(BF16), r.value_in[i])
    r.entry[...] = jnp.zeros_like(r.entry)
    for d in range(1, NZ):

        @pl.when(z >= d)
        def _(d=d):
            await_copy(r.total_in.at[ring_z(-d)], r.total_s.at[d], r.total_r.at[d], on_z(d))
            r.entry[...] += power(4 * (d - 1)) * r.total_in[ring_z(-d)].astype(F32)

    incoming = r.entry[...]
    fade = jnp.exp(-own_rate * (position + 1.0))
    for i in range(NY):
        mixed = r.intra[i] + fade * dot(r.query_in[i], incoming.astype(BF16))
        incoming = power(1) * incoming + r.local[i]
        mean = jnp.mean(mixed * mixed, axis=-1, keepdims=True)
        out = (mixed * lax.rsqrt(mean + EPSILON)).astype(BF16)
        r.heads[y, i] = out.reshape(4, 2, 16, 128)
    for d in (2, 1, 3):
        launch(remote(r.heads.at[y], r.heads.at[y], r.heads_s.at[d], r.heads_r.at[d], on_y(d)))
    z_wait(2)
    z_step(3)

    def heads_wait(d):
        await_copy(r.heads.at[ring_y(-d)], r.heads_s.at[d], r.heads_r.at[d], on_y(d))

    z_wait(3)
    z_step(4)
    swap((2,), range(6))
    heads_wait(1)
    heads_wait(3)
    heads_wait(2)
    swap((0, 1), (2, 3, 4))
    z_wait(4)

    def project(which, n):
        lhs = jnp.concatenate([r.heads[h, :, :, which].reshape(256, 128) for h in range(4)], axis=1)
        rhs = r.proj[4 * n : 4 * (n + 1)].reshape(384, 512)
        return nt_dot(lhs, rhs).reshape(4, 4, 16, 384)

    pair_copies = []
    for n in range(2):
        r.pair_out[n] = project(1 - c, n).astype(BF16)
        pair_copies.append(
            remote(r.pair_out.at[n], r.pair_in.at[n], r.pair_s.at[n], r.pair_r.at[n], partner)
        )
        launch(pair_copies[n])
    for n in range(2):
        r.part[n] = project(c, n)
    for n in range(2):
        pair_copies[n].wait_recv()
        both = r.part[n] + r.pair_in[n].astype(F32)
        r.part[n] = both
        r.part_out[n] = both.astype(BF16)
        for d in (2, 1, 3):
            launch(
                remote(
                    r.part_out.at[n, :, ring_x(d)],
                    r.part_in.at[n, x],
                    r.part_s.at[n, d],
                    r.part_r.at[n, d],
                    on_x(d),
                )
            )
    pass_on((0, 1), (0, 1))
    for n in range(2):
        slab = r.part[n, :, x]
        for d in (1, 3, 2):
            await_copy(r.part_in.at[n, ring_x(-d)], r.part_s.at[n, d], r.part_r.at[n, d], on_x(d))
            slab = slab + r.part_in[n, ring_x(-d)].astype(F32)
        r.slab[n] = slab
        r.slab_out[n] = slab.astype(BF16)
        for d in (2, 1, 3):
            launch(
                remote(
                    r.slab_out.at[n, ring_y(d)],
                    r.slab_in.at[n, y],
                    r.slab_s.at[n, d],
                    r.slab_r.at[n, d],
                    on_y(d),
                )
            )
    for n in range(2):
        for d in (1, 3, 2):
            await_copy(r.slab_in.at[n, ring_y(-d)], r.slab_s.at[n, d], r.slab_r.at[n, d], on_y(d))
            r.slab[n, ring_y(-d)] = r.slab_in[n, ring_y(-d)].astype(F32)
    swap((0, 1), (5,))
    attended = jnp.concatenate(
        [
            r.slab[zz // 4, yy][:, SHARD * (zz % 4) : SHARD * (zz % 4 + 1)]
            for zz in range(NZ)
            for yy in range(NY)
        ],
        axis=1,
    )
    hidden = r.stream[...].astype(F32) + attended
    r.hidden[...] = hidden
    mean = jnp.mean(hidden * hidden, axis=-1, keepdims=True)
    r.tokens[x, c] = (hidden * lax.rsqrt(mean + EPSILON) * r.gain[...]).astype(BF16)
    square = lax.broadcasted_iota(jnp.int32, (16, 16), 0) == lax.broadcasted_iota(
        jnp.int32, (16, 16), 1
    )

    def upright(row):
        wide = jnp.where(square, jnp.broadcast_to(row, (16, 16)).astype(F32), 0.0)
        return jnp.sum(wide, axis=1, keepdims=True)

    table_lane = lax.broadcasted_iota(jnp.int32, (16, 128), 1)
    r.tables[x, c] = jnp.where(
        table_lane == 0, upright(r.routes[0:1, :]), upright(r.routes[1:2, :])
    ).astype(jnp.int32)

    for d in (2, 1, 3, 0):
        for n, ref in enumerate((r.tokens, r.tables)):

            def make(d=d, n=n, ref=ref):
                block = ref.at[x, c]
                device = at(z, y, ring_x(d), core)
                return remote(block, block, r.tok_s.at[n, d], r.tok_r.at[n, d, c], device)

            if d:
                launch(make())
            else:
                launch_if(jnp.logical_not(source), make)

    pass_on((0, 1), (2, 3, 4))

    near = zl // 2
    edge = (zl * zl - 3 * zl + 2) // 2
    cross_to = at(lax.rem(4 * half + 7 - 3 * near, NZ), y, x, c)

    def lanes_of(ref, q):
        return ref.at[:, pl.ds(768 * q, 768)]

    def cross_copy(t, q):
        return remote(
            lanes_of(r.cross.at[t], q),
            lanes_of(r.line.at[t, 3 - near], q),
            r.cross_s.at[t, q],
            r.line_r.at[t, 3 - near, q],
            cross_to,
        )

    low_lane = lax.broadcasted_iota(jnp.int32, (128, CHUNK), 1) < SLOTS

    def expert_of(rel, t):
        return x * 4 + t * 2 + (half if rel == 0 else 1 - half)

    @pl.when(source)
    def _():
        for d in (0, 1, 3, 2):
            for n, ref in enumerate((r.tokens, r.tables)):
                for other in range(2):
                    if d == 0 and other == 1:
                        continue
                    cc = 1 - c if d == 0 else other
                    block = ref.at[ring_x(-d), cc]
                    await_copy(block, r.tok_s.at[n, d], r.tok_r.at[n, d, cc], on_x(d))
        rows = r.tokens[...].reshape(128, DM)
        table = r.tables[...].reshape(128, 128)
        first, second = table[:, 0:1], table[:, 1:2]
        lanes = lax.broadcasted_iota(jnp.int32, (128, 128), 1)
        earlier = (lanes < lax.broadcasted_iota(jnp.int32, (128, 128), 0)).astype(BF16)
        pairs = [(1, 0), (1, 1), (0, 0), (0, 1)]
        hits = []
        for rel, t in pairs:
            expert = expert_of(rel, t)
            hits.append(jnp.where(jnp.logical_or(first == expert, second == expert), 1.0, 0.0))
        wide = jnp.zeros((128, 128), F32)
        for n, hit in enumerate(hits):
            wide = jnp.where(lanes == n, hit, wide)
        ranks = dot(earlier, wide.astype(BF16)).astype(jnp.int32)
        slot = lax.broadcasted_iota(jnp.int32, (128, CHUNK), 1)
        lows, highs = [], []
        for n, (rel, t) in enumerate(pairs):
            rank = ranks[:, n : n + 1]
            low = jnp.where(slot == rank, hits[n], 0.0)
            low = jnp.where(low_lane, low, 0.0).astype(BF16)
            high = jnp.where(slot - SLOTS == rank, hits[n], 0.0).astype(BF16)
            r.sel[rel, t, 0] = low
            r.sel[rel, t, 1] = high
            lows.append(low)
            highs.append(high)
        for n in range(2):
            low = jnp.concatenate(lows[2 * n : 2 * n + 2], axis=1)
            high = jnp.concatenate(highs[2 * n : 2 * n + 2], axis=1)
            both = (tn_dot(low, rows[:, :HALF]) + tn_dot(high, rows[:, HALF:])).astype(BF16)
            for t in range(2):
                chunk = both[CHUNK * t : CHUNK * (t + 1)]
                if n == 0:
                    r.cross[t] = chunk
                    for q in range(2):
                        cross_copy(t, q).start()
                else:
                    r.line[t, near] = chunk

    order = [
        near,
        edge * (2 + near) + (1 - edge) * (1 - near),
        edge * (1 - near) + (1 - edge) * (2 + near),
        3 - near,
    ]

    def origin(s):
        outer = s // 2
        return (1 - outer) * (c + 2 * s) + outer * (5 * s - 11)

    def spread(i):
        s = order[i]
        o = origin(s)
        for t in range(2):
            block = r.line.at[t, s]
            for q in range(2):
                piece = lanes_of(block, q)
                if i > 0:
                    await_copy(piece, r.line_s.at[0, t, s, q], r.line_r.at[t, s, q], on_z(1))
                else:

                    @pl.when(jnp.logical_not(source))
                    def _(t=t, q=q, piece=piece):
                        await_copy(piece, r.line_s.at[0, t, s, q], r.line_r.at[t, s, q], on_z(1))

                for side, condition in (
                    (0, jnp.logical_and(o <= zl, zl < 3)),
                    (1, jnp.logical_and(o >= zl, zl > 0)),
                ):
                    launch_if(
                        condition,
                        lambda piece=piece, t=t, s=s, q=q, side=side: remote(
                            piece,
                            piece,
                            r.line_s.at[side, t, s, q],
                            r.line_r.at[t, s, q],
                            on_z(-1 if side else 1),
                        ),
                    )
            for j, d, wanted in ((0, 2, role == t), (1, 1, role != t), (2, -1, role != t)):
                launch_if(
                    wanted,
                    lambda block=block, s=s, j=j, d=d: remote(
                        block, r.got.at[j, s], r.got_s.at[j, s], r.got_r.at[j, s], on_y(d)
                    ),
                )

    spread(0)
    spread(1)
    pass_on((0, 1), (5,))
    pass_on((2,), range(6))
    spread(2)
    spread(3)

    @pl.when(source)
    def _():
        logits = nt_dot(r.tokens[...].reshape(128, DM), r.router[...])
        table = r.tables[...].reshape(128, 128)
        first, second = table[:, 0:1], table[:, 1:2]
        expert = lax.broadcasted_iota(jnp.int32, logits.shape, 1)

        def lifted(chosen):
            logit = jnp.sum(jnp.where(expert == chosen, logits, 0.0), axis=1, keepdims=True)
            return jax.nn.sigmoid(logit)

        lift_first, lift_second = lifted(first), lifted(second)
        both = lift_first + lift_second
        for rel in range(2):
            for t in range(2):
                chosen = expert_of(rel, t)
                share = jnp.where(first == chosen, lift_first / both, 0.0) + jnp.where(
                    second == chosen, lift_second / both, 0.0
                )
                r.share[rel, t] = jnp.broadcast_to(share, (128, 128))

    other, side_end, far_end = 1 - near, 2 + near, 3 - near

    def arrived(p):
        for j, d in ((0, 2), (1, 1), (2, -1)):
            await_copy(r.got.at[j, p], r.got_s.at[j, p], r.got_r.at[j, p], on_y(d))

    def compute(which):
        chunks = []
        for p in which:
            chunks += [r.line[role, p]] + [r.got[j, p] for j in range(3)]
        for n in range(4):
            a, b = chunks[2 * n].astype(F32), chunks[2 * n + 1].astype(F32)
            rows = slice(CHUNK * n, CHUNK * (n + 1))
            r.flat[rows, :HALF] = jnp.concatenate([a[:SLOTS], b[:SLOTS]], axis=0).astype(BF16)
            r.flat[rows, HALF:] = jnp.concatenate([a[SLOTS:], b[SLOTS:]], axis=0).astype(BF16)
        rows = r.flat[...]
        gated = nt_dot(rows, r.gate[...])
        inner = (gated * jax.nn.sigmoid(gated) * nt_dot(rows, r.up[...])).astype(BF16)
        left = dot(inner, r.down[:, :HALF])
        right = dot(inner, r.down[:, HALF:])
        for n, p in enumerate(which):
            for j in range(4):
                rows = slice(SLOTS * (4 * n + j), SLOTS * (4 * n + j + 1))
                r.partial[j, p] = jnp.concatenate([left[rows], right[rows]], axis=0).astype(BF16)

    def give_back(p):
        for j, d in ((0, 2), (1, -1), (2, 1)):
            launch(
                remote(
                    r.partial.at[j + 1, p], r.back.at[j, p], r.back_s.at[j, p], r.back_r.at[j, p], on_y(d)
                )
            )

    arrived(near)
    arrived(other)
    weights_ready()
    compute((near, other))
    give_back(other)
    arrived(side_end)
    arrived(far_end)
    compute((far_end, side_end))
    for p in (far_end, side_end, near):
        give_back(p)

    def collect(p):
        for j, d in ((0, 2), (1, 1), (2, -1)):
            await_copy(r.back.at[j, p], r.back_s.at[j, p], r.back_r.at[j, p], on_y(d))
        r.total[role, p] = r.partial[0, p].astype(F32) + r.back[0, p].astype(F32)
        r.total[1 - role, p] = r.back[1, p].astype(F32) + r.back[2, p].astype(F32)

    ends = (at(lax.rem(4 * half + 4 + c, NZ), y, x, c), at(lax.rem(4 * half + 6 + c, NZ), y, x, c))

    def along(s):
        o = origin(s)
        for t in range(2):
            for q in range(2):
                cols = slice(768 * q, 768 * (q + 1))
                out = lanes_of(r.line_out.at[t, s], q)

                def add_line(side, t=t, q=q, cols=cols):
                    block = lanes_of(r.line_in.at[side, t, s], q)
                    await_copy(block, r.sum_s.at[t, s, q], r.sum_r.at[side, t, s, q], on_z(1))
                    r.total[t, s, :, cols] += r.line_in[side, t, s, :, cols].astype(F32)

                @pl.when(jnp.logical_and(o >= zl, zl > 0))
                def _(add_line=add_line):
                    add_line(0)

                @pl.when(jnp.logical_and(o <= zl, zl < 3))
                def _(add_line=add_line):
                    add_line(1)

                r.line_out[t, s, :, cols] = r.total[t, s, :, cols].astype(BF16)
                for side, wanted, last in ((0, o > zl, zl == 3), (1, o < zl, zl == 0)):
                    launch_if(
                        jnp.logical_and(wanted, jnp.logical_not(last)),
                        lambda out=out, t=t, s=s, q=q, side=side: remote(
                            out,
                            lanes_of(r.line_in.at[side, t, s], q),
                            r.sum_s.at[t, s, q],
                            r.sum_r.at[side, t, s, q],
                            on_z(-1 if side else 1),
                        ),
                    )
                    launch_if(
                        jnp.logical_and(wanted, last),
                        lambda out=out, t=t, s=s, q=q, side=side: remote(
                            out,
                            lanes_of(r.ret.at[t], q),
                            r.sum_s.at[t, s, q],
                            r.ret_r.at[t, q],
                            ends[side],
                        ),
                    )

    for p in (other, far_end, side_end, near):
        collect(p)
        along(p)

    def home_copy(side, d, cc):
        cols = pl.ds(HALF * side, HALF)
        return remote(
            r.home_out.at[ring_x(d), cc, :, cols],
            r.home_in.at[x, :, cols],
            r.home_s.at[side, d, cc],
            r.home_r.at[side, d],
            at(z, y, ring_x(d), cc),
        )

    home_targets = [(d, other) for d in (2, 1, 3) for other in range(2)] + [(0, 1 - c)]

    @pl.when(source)
    def _():
        for side in range(2):
            cols = slice(HALF * side, HALF * (side + 1))
            value = None
            for rel in range(2):
                for t in range(2):
                    if rel == 1 and side == 0:
                        for q in range(2):
                            block = lanes_of(r.ret.at[t], q)
                            await_copy(block, r.sum_s.at[t, 0, q], r.ret_r.at[t, q], ends[0])
                    rows = r.ret[t] if rel else r.line_out[t, near]
                    term = r.share[rel, t][:, 0:1] * dot(r.sel[rel, t, side], rows)
                    value = term if value is None else value + term
            value = value.reshape(4, 2, 16, HALF)
            r.mixed[:, :, :, cols] = value
            r.home_out[:, :, :, cols] = value.astype(BF16)
            for d, cc in home_targets:
                home_copy(side, d, cc).start()
        r.home[...] = r.mixed[x, c]

    def home_wait(d):
        for side in range(2):
            cols = pl.ds(HALF * side, HALF)
            block = r.home_in.at[ring_x(-d), :, cols]
            await_copy(block, r.home_s.at[side, d, c], r.home_r.at[side, d], on_x(d))

    @pl.when(jnp.logical_not(source))
    def _():
        home_wait(0)
        r.home[...] = r.home_in[x].astype(F32)

    result = r.hidden[...] + r.home[...]
    for d in (1, 3, 2):
        home_wait(d)
        result = result + r.home_in[ring_x(-d)].astype(F32)
    r.out[...] = result.astype(BF16)

    @pl.when(source)
    def _():
        for t in range(2):
            for q in range(2):
                cross_copy(t, q).wait_send()
        for side in range(2):
            for d, cc in home_targets:
                home_copy(side, d, cc).wait_send()

    for condition, make in guarded:

        @pl.when(condition)
        def _(make=make):
            make().wait_send()

    for copy in sends:
        copy.wait_send()


VMEM = pl.BlockSpec(memory_space=pltpu.VMEM)
ANY = pl.BlockSpec(memory_space=pl.ANY)


def body(
    stream,
    query,
    key,
    value,
    decay_rate,
    out_weight,
    norm_gain,
    router_weight,
    routes,
    expert_gate,
    expert_up,
    expert_down,
):
    return pl.pallas_call(
        kernel,
        out_shape=jax.ShapeDtypeStruct(stream.shape, BF16),
        in_specs=[VMEM] * 9 + [ANY] * 3,
        out_specs=VMEM,
        scratch_shapes=list(SCRATCH.values()),
        compiler_params=pltpu.CompilerParams(
            collective_id=0, has_side_effects=True, vmem_limit_bytes=56 * 2**20
        ),
        name="whole",
    )(
        stream,
        query,
        key,
        value,
        decay_rate.reshape(1, 4),
        out_weight.T,
        norm_gain.reshape(1, DM),
        routes.T,
        router_weight.T,
        expert_gate.T,
        expert_up.T,
        expert_down,
    )


def solution(mesh):
    placed = (
        P(("ctx", "ep"), None),
        P("ctx", "ep"),
        P("ctx", "ep"),
        P("ctx", "ep"),
        P("ep"),
        P("ep", "ctx"),
        P(),
        P(),
        P(("ctx", "ep"), None),
        P(None, ("ep", "ctx")),
        P(None, ("ep", "ctx")),
        P(("ep", "ctx"), None),
    )
    return jax.shard_map(
        body, mesh=mesh, in_specs=placed, out_specs=P(("ctx", "ep"), None), check_vma=False
    )
```

time: 157 us -> 136 us (0.87); the launches traced: 157 us -> 134 us
  Pallas kernels: 155 us -> 132 us
    pallas_call x1, Pallas kernels: 155 us -> 132 us  [body(): pl.pallas_call(kernel, out_shape=jax.ShapeDtypeStruct(stream.shape, BF16)...]
where the time goes in v3:
time: 136 us; the launch traced here: 134 us
  Pallas kernels  132 us (97%)
  local copies, waits for them, and re-layouts  1.54 us (1%)
    pallas_call x1, Pallas kernels, body(): pl.pallas_call(kernel, out_shape=jax.ShapeDtypeStruct(stream.shape, BF16)...  132 us

profile of v3, /device:TPU:1, one launch (start us, length us, event | category | flops | bytes accessed | tf_op | source)
XLA Modules:
  0.0 133.8 jit_solution(2444827570577641904)
XLA Ops:
  0.0 132.2 %whole.1 = bf16[16,3072]{1,0:T(8,128)(2,1)} custom-call(bf16[16,3072]{1,0:T(8,128)(2,1)} %refs_0_.1, bf16[128,512]{1,0:T(8,128)(2,1)} %refs_1_.1, bf16[128,512]{1,0:T(8,128)(2,1)} %refs_2_.1, bf16[128,512]{1,0:T(8,128)(2,1)} %refs_3_.1, f32[1,4]{1,0:T(1,128)} %bitcast.13, bf16[96,512]{1,0:T(8,128)(2,1)} %bitcast.9, f32[1,3072]{1,0:T(1,128)} %bitcast.11, ...), custom_call_target="tpu_custom_call" | custom-call | tf_op jit(solution)/shard_map/whole/pallas_call | solution.py:823
  132.2 1.5 %copy.14 = bf16[16,3072]{1,0:T(8,128)(2,1)} copy(bf16[16,3072]{1,0:T(8,128)(2,1)} %whole.1) | data formatting | bytes 196608

commit v4 on v3

--- a/solution.py
+++ b/solution.py
@@ -18,6 +18,8 @@
 CHUNK = 48
 SHARD = 96
 HIDDEN = 288
+PIECES = 2
+WIDTH = HALF // PIECES
 PIECE = 96
 PART = 48
 
@@ -58,8 +60,8 @@
     slab_out=bf(2, 4, 16, 384),
     slab_in=bf(2, 4, 16, 384),
     hidden=fl(16, DM),
-    tokens=bf(4, 2, 16, DM),
-    tables=pltpu.VMEM((4, 2, 16, 128), jnp.int32),
+    tokens=bf(8, 16, DM),
+    tables=pltpu.VMEM((8, 16, 128), jnp.int32),
     gate=bf(2 * HIDDEN, DM),
     up=bf(2 * HIDDEN, DM),
     down=bf(2 * HIDDEN, DM),
@@ -79,25 +81,13 @@
     home_out=bf(4, 2, 16, DM),
     home_in=bf(4, 16, DM),
     home=fl(16, DM),
-    load_sem=dma(3),
-    block_s=dma(3, 4), block_r=dma(3, 4),
-    total_s=dma(8), total_r=dma(8),
-    proj_s=dma(2, 5), proj_r=dma(2, 5),
-    heads_s=dma(4), heads_r=dma(4),
-    pair_s=dma(2), pair_r=dma(2),
-    part_s=dma(2, 4), part_r=dma(2, 4),
-    slab_s=dma(2, 4), slab_r=dma(2, 4),
-    tok_s=dma(2, 4), tok_r=dma(2, 4, 2),
-    own_s=dma(3), own_r=dma(3),
-    swap_s=dma(3, 2, 3), swap_r=dma(3, 2, 3),
-    pass_s=dma(3, 2, 3), pass_r=dma(3, 2, 3),
-    cross_s=dma(2, 2),
-    line_s=dma(2, 2, 4, 2), line_r=dma(2, 4, 2),
-    got_s=dma(3, 4), got_r=dma(3, 4),
-    back_s=dma(3, 4), back_r=dma(3, 4),
-    sum_s=dma(2, 4, 2), sum_r=dma(2, 2, 4, 2),
-    ret_r=dma(2, 2),
-    home_s=dma(2, 4, 2), home_r=dma(2, 4),
+    early_s=dma(1), slab_s=dma(1), tok_s=dma(4), total_s=dma(1), own_s=dma(2),
+    swap_s=dma(2), pass_s=dma(2), cross_s=dma(1), line_s=dma(1), row_s=dma(1), sum_s=dma(1),
+    home_s=dma(1),
+    block_r=dma(4), total_r=dma(1), proj_r=dma(4), heads_r=dma(1), pair_r=dma(2), part_r=dma(2),
+    slab_r=dma(1), tok_r=dma(2), own_r=dma(2), swap_r=dma(4), pass_r=dma(2),
+    line_r=dma(2, 4, PIECES), got_r=dma(4), back_r=dma(4), sum_r=dma(2, 5, PIECES), ret_r=dma(1),
+    home_r=dma(2),
 )
 
 
@@ -122,8 +112,8 @@
     )
 
 
-def await_copy(dst, send, recv, device):
-    remote(dst, dst, send, recv, device).wait_recv()
+def await_bytes(ref, semaphore):
+    pltpu.make_async_copy(ref, ref, semaphore).wait()
 
 
 def greet(barrier, devices):
@@ -185,19 +175,17 @@
     greet(barrier, [on_x(d) for d in range(1, NX)])
     greet(barrier, [at(z, y, ring_x(d), 1 - c) for d in range(NX)])
     greet(barrier, swap_to)
-    sends = []
-    guarded = []
 
     def launch(copy):
         copy.start()
-        sends.append(copy)
 
     def launch_if(condition, make):
         @pl.when(condition)
         def _():
             make().start()
 
-        guarded.append((condition, make))
+    def units(n):
+        return r.gate.at[pl.ds(0, 16 * n)]
 
     experts = ((r.gate_hbm, r.gate), (r.up_hbm, r.up), (r.down_hbm, r.down))
     own_rows = pl.ds(0, HIDDEN)
@@ -207,7 +195,7 @@
 
     def load(m):
         hbm, ref = experts[m]
-        return pltpu.make_async_copy(hbm, ref.at[own_rows], r.load_sem.at[m])
+        return pltpu.make_async_copy(hbm, ref.at[own_rows], r.own_r.at[m // 2])
 
     @pl.when(keeper)
     def _():
@@ -215,60 +203,42 @@
             load(m).start()
 
     away = jnp.logical_not(keeper)
-    back_side = (1, 0, 2)
-
-    def swap(sides, units):
-        for unit in units:
-            m, k = divmod(unit, 2)
-            for side in sides:
+    batches = (((0, 1), (0, 1)), ((0, 1), (2, 3, 4)), ((0, 1), (5,)), ((2,), range(6)))
+
+    def parts(batch):
+        sides, numbers = batches[batch]
+        return [(number // 2, number % 2, side) for number in numbers for side in sides]
+
+    def swap(batch, numbers=range(6)):
+        for m, k, side in parts(batch):
+            if m * 2 + k in numbers:
                 launch_if(
                     away,
                     lambda m=m, k=k, side=side: remote(
                         experts[m][0].at[part_rows(0, k, side)],
                         experts[m][1].at[part_rows(HIDDEN, k, side)],
-                        r.swap_s.at[m, k, side],
-                        r.swap_r.at[m, k, side],
+                        r.swap_s.at[side // 2],
+                        r.swap_r.at[batch],
                         swap_to[side],
                     ),
                 )
 
-    def pass_on(sides, units):
-        for unit in units:
-            m, k = divmod(unit, 2)
-            for side in sides:
+    def pass_on(batch):
+        @pl.when(away)
+        def _():
+            await_bytes(units(3 * len(parts(batch))), r.swap_r.at[batch])
+            for m, k, side in parts(batch):
                 ref = experts[m][1].at[part_rows(HIDDEN, k, side)]
-
-                @pl.when(away)
-                def _(m=m, k=k, side=side, ref=ref):
-                    await_copy(
-                        ref,
-                        r.swap_s.at[m, k, side],
-                        r.swap_r.at[m, k, side],
-                        swap_to[back_side[side]],
-                    )
-
-                launch_if(
-                    away,
-                    lambda m=m, k=k, side=side, ref=ref: remote(
-                        ref, ref, r.pass_s.at[m, k, side], r.pass_r.at[m, k, side], partner
-                    ),
-                )
+                remote(ref, ref, r.pass_s.at[side // 2], r.pass_r.at[side // 2], partner).start()
 
     def weights_ready():
+        await_bytes(r.gate, r.own_r.at[0])
+        await_bytes(r.gate.at[own_rows], r.own_r.at[1])
+
         @pl.when(keeper)
         def _():
-            for m in range(3):
-                load(m).wait()
-                for k in range(2):
-                    for side in range(3):
-                        ref = experts[m][1].at[part_rows(HIDDEN, k, side)]
-                        await_copy(ref, r.pass_s.at[m, k, side], r.pass_r.at[m, k, side], partner)
-
-        @pl.when(away)
-        def _():
-            for m in range(3):
-                ref = experts[m][1].at[own_rows]
-                await_copy(ref, r.own_s.at[m], r.own_r.at[m], partner)
+            await_bytes(r.gate, r.pass_r.at[0])
+            await_bytes(r.gate.at[own_rows], r.pass_r.at[1])
 
     rates = r.rates[...]
     length = r.query.shape[0]
@@ -298,14 +268,11 @@
                 remote(
                     whole.at[:, head_columns(ring_y(d))],
                     own.at[y],
-                    r.block_s.at[n, d],
-                    r.block_r.at[n, d],
+                    r.early_s.at[0],
+                    r.block_r.at[0 if n == 2 else d],
                     on_y(d),
                 )
             )
-
-    def block_wait(n, d):
-        await_copy(blocks[n][1].at[ring_y(-d)], r.block_s.at[n, d], r.block_r.at[n, d], on_y(d))
 
     def z_parts(k):
         if k < 4:
@@ -314,36 +281,30 @@
 
     def z_step(k):
         a, b = z_parts(k)
-        launch(remote(a, a, r.proj_s.at[0, k], r.proj_r.at[0, k], on_z(1)))
-        launch(remote(b, b, r.proj_s.at[1, k], r.proj_r.at[1, k], on_z(-1)))
+        launch(remote(a, a, r.early_s.at[0], r.proj_r.at[k - 1], on_z(1)))
+        launch(remote(b, b, r.early_s.at[0], r.proj_r.at[k - 1], on_z(-1)))
 
     def z_wait(k):
-        if k < 4:
-            a, b = r.proj.at[ring_z(-k)], r.proj.at[ring_z(k)]
-        else:
-            a, b = r.proj.at[ring_z(4)].at[pl.ds(0, 48)], r.proj.at[ring_z(4)].at[pl.ds(48, 48)]
-        await_copy(a, r.proj_s.at[0, k], r.proj_r.at[0, k], on_z(1))
-        await_copy(b, r.proj_s.at[1, k], r.proj_r.at[1, k], on_z(-1))
+        await_bytes(r.proj.at[pl.ds(0, 2 if k < 4 else 1)], r.proj_r.at[k - 1])
 
     z_step(1)
-    swap((0, 1), (0,))
+    swap(0, (0,))
     for m in range(3):
         launch_if(
             keeper,
             lambda m=m: remote(
-                experts[m][0], experts[m][1].at[own_rows], r.own_s.at[m], r.own_r.at[m], partner
+                experts[m][0], experts[m][1].at[own_rows], r.own_s.at[m // 2], r.own_r.at[m // 2], partner
             ),
         )
 
     fade = jnp.exp(-own_rate * (length - 1.0 - position))
     for d in (0, 1, 3, 2):
         if d:
-            block_wait(0, d)
-            block_wait(1, d)
+            await_bytes(r.key_in.at[pl.ds(0, 2)], r.block_r.at[d])
         i = ring_y(-d)
         faded = (r.key_in[i].astype(F32) * fade).astype(BF16)
         r.local[i] = tn_dot(faded, r.value_in[i])
-    swap((0, 1), (1,))
+    swap(0, (1,))
     total = r.local[3]
     for i in range(3):
         total = total + power(3 - i) * r.local[i]
@@ -352,24 +313,27 @@
         launch_if(
             z + d < NZ,
             lambda d=d: remote(
-                r.total_out, r.total_in.at[z], r.total_s.at[d], r.total_r.at[d], on_z(d)
+                r.total_out, r.total_in.at[z], r.total_s.at[0], r.total_r.at[0], on_z(d)
             ),
         )
     z_wait(1)
     z_step(2)
     decay = jnp.where(gap >= 0, jnp.exp(-own_rate * jnp.maximum(gap, 0.0)), 0.0)
-    for d in (0, 1, 3, 2):
-        if d:
-            block_wait(2, d)
-        i = ring_y(-d)
+    await_bytes(r.key_in.at[pl.ds(0, 3)], r.block_r.at[0])
+    for i in range(NY):
         scores = nt_dot(r.query_in[i], r.key_in[i])
         r.intra[i] = dot((scores * decay).astype(BF16), r.value_in[i])
     r.entry[...] = jnp.zeros_like(r.entry)
     for d in range(1, NZ):
 
+        @pl.when(z == d)
+        def _(d=d):
+            await_bytes(r.total_in.at[pl.ds(0, d)], r.total_r.at[0])
+
+    for d in range(1, NZ):
+
         @pl.when(z >= d)
         def _(d=d):
-            await_copy(r.total_in.at[ring_z(-d)], r.total_s.at[d], r.total_r.at[d], on_z(d))
             r.entry[...] += power(4 * (d - 1)) * r.total_in[ring_z(-d)].astype(F32)
 
     incoming = r.entry[...]
@@ -381,20 +345,15 @@
         out = (mixed * lax.rsqrt(mean + EPSILON)).astype(BF16)
         r.heads[y, i] = out.reshape(4, 2, 16, 128)
     for d in (2, 1, 3):
-        launch(remote(r.heads.at[y], r.heads.at[y], r.heads_s.at[d], r.heads_r.at[d], on_y(d)))
+        launch(remote(r.heads.at[y], r.heads.at[y], r.early_s.at[0], r.heads_r.at[0], on_y(d)))
     z_wait(2)
     z_step(3)
 
-    def heads_wait(d):
-        await_copy(r.heads.at[ring_y(-d)], r.heads_s.at[d], r.heads_r.at[d], on_y(d))
-
     z_wait(3)
     z_step(4)
-    swap((2,), range(6))
-    heads_wait(1)
-    heads_wait(3)
-    heads_wait(2)
-    swap((0, 1), (2, 3, 4))
+    swap(3)
+    await_bytes(r.heads.at[pl.ds(0, 3)], r.heads_r.at[0])
+    swap(1)
     z_wait(4)
 
     def project(which, n):
@@ -402,17 +361,13 @@
         rhs = r.proj[4 * n : 4 * (n + 1)].reshape(384, 512)
         return nt_dot(lhs, rhs).reshape(4, 4, 16, 384)
 
-    pair_copies = []
     for n in range(2):
         r.pair_out[n] = project(1 - c, n).astype(BF16)
-        pair_copies.append(
-            remote(r.pair_out.at[n], r.pair_in.at[n], r.pair_s.at[n], r.pair_r.at[n], partner)
-        )
-        launch(pair_copies[n])
+        launch(remote(r.pair_out.at[n], r.pair_in.at[n], r.early_s.at[0], r.pair_r.at[n], partner))
     for n in range(2):
         r.part[n] = project(c, n)
     for n in range(2):
-        pair_copies[n].wait_recv()
+        await_bytes(r.pair_in.at[n], r.pair_r.at[n])
         both = r.part[n] + r.pair_in[n].astype(F32)
         r.part[n] = both
         r.part_out[n] = both.astype(BF16)
@@ -421,16 +376,16 @@
                 remote(
                     r.part_out.at[n, :, ring_x(d)],
                     r.part_in.at[n, x],
-                    r.part_s.at[n, d],
-                    r.part_r.at[n, d],
+                    r.early_s.at[0],
+                    r.part_r.at[n],
                     on_x(d),
                 )
             )
-    pass_on((0, 1), (0, 1))
+    pass_on(0)
     for n in range(2):
         slab = r.part[n, :, x]
+        await_bytes(r.part_in.at[n, pl.ds(0, 3)], r.part_r.at[n])
         for d in (1, 3, 2):
-            await_copy(r.part_in.at[n, ring_x(-d)], r.part_s.at[n, d], r.part_r.at[n, d], on_x(d))
             slab = slab + r.part_in[n, ring_x(-d)].astype(F32)
         r.slab[n] = slab
         r.slab_out[n] = slab.astype(BF16)
@@ -439,16 +394,16 @@
                 remote(
                     r.slab_out.at[n, ring_y(d)],
                     r.slab_in.at[n, y],
-                    r.slab_s.at[n, d],
-                    r.slab_r.at[n, d],
+                    r.slab_s.at[0],
+                    r.slab_r.at[0],
                     on_y(d),
                 )
             )
+    await_bytes(r.slab_in.at[:, pl.ds(0, 3)], r.slab_r.at[0])
     for n in range(2):
         for d in (1, 3, 2):
-            await_copy(r.slab_in.at[n, ring_y(-d)], r.slab_s.at[n, d], r.slab_r.at[n, d], on_y(d))
             r.slab[n, ring_y(-d)] = r.slab_in[n, ring_y(-d)].astype(F32)
-    swap((0, 1), (5,))
+    swap(2)
     attended = jnp.concatenate(
         [
             r.slab[zz // 4, yy][:, SHARD * (zz % 4) : SHARD * (zz % 4 + 1)]
@@ -460,7 +415,7 @@
     hidden = r.stream[...].astype(F32) + attended
     r.hidden[...] = hidden
     mean = jnp.mean(hidden * hidden, axis=-1, keepdims=True)
-    r.tokens[x, c] = (hidden * lax.rsqrt(mean + EPSILON) * r.gain[...]).astype(BF16)
+    r.tokens[ep] = (hidden * lax.rsqrt(mean + EPSILON) * r.gain[...]).astype(BF16)
     square = lax.broadcasted_iota(jnp.int32, (16, 16), 0) == lax.broadcasted_iota(
         jnp.int32, (16, 16), 1
     )
@@ -470,7 +425,7 @@
         return jnp.sum(wide, axis=1, keepdims=True)
 
     table_lane = lax.broadcasted_iota(jnp.int32, (16, 128), 1)
-    r.tables[x, c] = jnp.where(
+    r.tables[ep] = jnp.where(
         table_lane == 0, upright(r.routes[0:1, :]), upright(r.routes[1:2, :])
     ).astype(jnp.int32)
 
@@ -478,29 +433,29 @@
         for n, ref in enumerate((r.tokens, r.tables)):
 
             def make(d=d, n=n, ref=ref):
-                block = ref.at[x, c]
+                block = ref.at[ep]
                 device = at(z, y, ring_x(d), core)
-                return remote(block, block, r.tok_s.at[n, d], r.tok_r.at[n, d, c], device)
+                return remote(block, block, r.tok_s.at[n if d else n + 2], r.tok_r.at[n], device)
 
             if d:
                 launch(make())
             else:
                 launch_if(jnp.logical_not(source), make)
 
-    pass_on((0, 1), (2, 3, 4))
+    pass_on(1)
 
     near = zl // 2
     edge = (zl * zl - 3 * zl + 2) // 2
     cross_to = at(lax.rem(4 * half + 7 - 3 * near, NZ), y, x, c)
 
     def lanes_of(ref, q):
-        return ref.at[:, pl.ds(768 * q, 768)]
+        return ref.at[:, pl.ds(WIDTH * q, WIDTH)]
 
     def cross_copy(t, q):
         return remote(
             lanes_of(r.cross.at[t], q),
             lanes_of(r.line.at[t, 3 - near], q),
-            r.cross_s.at[t, q],
+            r.cross_s.at[0],
             r.line_r.at[t, 3 - near, q],
             cross_to,
         )
@@ -512,14 +467,8 @@
 
     @pl.when(source)
     def _():
-        for d in (0, 1, 3, 2):
-            for n, ref in enumerate((r.tokens, r.tables)):
-                for other in range(2):
-                    if d == 0 and other == 1:
-                        continue
-                    cc = 1 - c if d == 0 else other
-                    block = ref.at[ring_x(-d), cc]
-                    await_copy(block, r.tok_s.at[n, d], r.tok_r.at[n, d, cc], on_x(d))
+        for n, ref in enumerate((r.tokens, r.tables)):
+            await_bytes(ref.at[pl.ds(0, 7)], r.tok_r.at[n])
         rows = r.tokens[...].reshape(128, DM)
         table = r.tables[...].reshape(128, 128)
         first, second = table[:, 0:1], table[:, 1:2]
@@ -553,7 +502,7 @@
                 chunk = both[CHUNK * t : CHUNK * (t + 1)]
                 if n == 0:
                     r.cross[t] = chunk
-                    for q in range(2):
+                    for q in range(PIECES):
                         cross_copy(t, q).start()
                 else:
                     r.line[t, near] = chunk
@@ -574,15 +523,15 @@
         o = origin(s)
         for t in range(2):
             block = r.line.at[t, s]
-            for q in range(2):
+            for q in range(PIECES):
                 piece = lanes_of(block, q)
                 if i > 0:
-                    await_copy(piece, r.line_s.at[0, t, s, q], r.line_r.at[t, s, q], on_z(1))
+                    await_bytes(piece, r.line_r.at[t, s, q])
                 else:
 
                     @pl.when(jnp.logical_not(source))
                     def _(t=t, q=q, piece=piece):
-                        await_copy(piece, r.line_s.at[0, t, s, q], r.line_r.at[t, s, q], on_z(1))
+                        await_bytes(piece, r.line_r.at[t, s, q])
 
                 for side, condition in (
                     (0, jnp.logical_and(o <= zl, zl < 3)),
@@ -593,7 +542,7 @@
                         lambda piece=piece, t=t, s=s, q=q, side=side: remote(
                             piece,
                             piece,
-                            r.line_s.at[side, t, s, q],
+                            r.line_s.at[0],
                             r.line_r.at[t, s, q],
                             on_z(-1 if side else 1),
                         ),
@@ -602,14 +551,14 @@
                 launch_if(
                     wanted,
                     lambda block=block, s=s, j=j, d=d: remote(
-                        block, r.got.at[j, s], r.got_s.at[j, s], r.got_r.at[j, s], on_y(d)
+                        block, r.got.at[j, s], r.row_s.at[0], r.got_r.at[s], on_y(d)
                     ),
                 )
 
     spread(0)
     spread(1)
-    pass_on((0, 1), (5,))
-    pass_on((2,), range(6))
+    pass_on(2)
+    pass_on(3)
     spread(2)
     spread(3)
 
@@ -635,20 +584,22 @@
                 r.share[rel, t] = jnp.broadcast_to(share, (128, 128))
 
     other, side_end, far_end = 1 - near, 2 + near, 3 - near
+    swapped = edge * (core - c) * (core - c)
+    third = side_end + swapped * (near - side_end)
+    fourth = near + swapped * (side_end - near)
 
     def arrived(p):
-        for j, d in ((0, 2), (1, 1), (2, -1)):
-            await_copy(r.got.at[j, p], r.got_s.at[j, p], r.got_r.at[j, p], on_y(d))
-
-    def compute(which):
-        chunks = []
-        for p in which:
-            chunks += [r.line[role, p]] + [r.got[j, p] for j in range(3)]
-        for n in range(4):
+        await_bytes(r.got.at[:, p], r.got_r.at[p])
+
+    def flatten(p, place):
+        chunks = [r.line[role, p]] + [r.got[j, p] for j in range(3)]
+        for n in range(2):
             a, b = chunks[2 * n].astype(F32), chunks[2 * n + 1].astype(F32)
-            rows = slice(CHUNK * n, CHUNK * (n + 1))
+            rows = slice(CHUNK * (2 * place + n), CHUNK * (2 * place + n + 1))
             r.flat[rows, :HALF] = jnp.concatenate([a[:SLOTS], b[:SLOTS]], axis=0).astype(BF16)
             r.flat[rows, HALF:] = jnp.concatenate([a[SLOTS:], b[SLOTS:]], axis=0).astype(BF16)
+
+    def compute(which):
         rows = r.flat[...]
         gated = nt_dot(rows, r.gate[...])
         inner = (gated * jax.nn.sigmoid(gated) * nt_dot(rows, r.up[...])).astype(BF16)
@@ -663,39 +614,46 @@
         for j, d in ((0, 2), (1, -1), (2, 1)):
             launch(
                 remote(
-                    r.partial.at[j + 1, p], r.back.at[j, p], r.back_s.at[j, p], r.back_r.at[j, p], on_y(d)
+                    r.partial.at[j + 1, p], r.back.at[j, p], r.row_s.at[0], r.back_r.at[p], on_y(d)
                 )
             )
 
     arrived(near)
+    flatten(near, 0)
+    weights_ready()
     arrived(other)
-    weights_ready()
+    flatten(other, 1)
     compute((near, other))
     give_back(other)
     arrived(side_end)
+    flatten(side_end, 1)
     arrived(far_end)
+    flatten(far_end, 0)
     compute((far_end, side_end))
-    for p in (far_end, side_end, near):
+    for p in (far_end, third, fourth):
         give_back(p)
 
     def collect(p):
-        for j, d in ((0, 2), (1, 1), (2, -1)):
-            await_copy(r.back.at[j, p], r.back_s.at[j, p], r.back_r.at[j, p], on_y(d))
+        await_bytes(r.back.at[:, p], r.back_r.at[p])
         r.total[role, p] = r.partial[0, p].astype(F32) + r.back[0, p].astype(F32)
         r.total[1 - role, p] = r.back[1, p].astype(F32) + r.back[2, p].astype(F32)
 
     ends = (at(lax.rem(4 * half + 4 + c, NZ), y, x, c), at(lax.rem(4 * half + 6 + c, NZ), y, x, c))
+
+    def stream(s, place, side):
+        here = 1 - lax.min(1, (origin(s) - place) * (origin(s) - place))
+        return s + here * side * (4 - s)
 
     def along(s):
         o = origin(s)
         for t in range(2):
-            for q in range(2):
-                cols = slice(768 * q, 768 * (q + 1))
+            for q in range(PIECES):
+                cols = slice(WIDTH * q, WIDTH * (q + 1))
                 out = lanes_of(r.line_out.at[t, s], q)
 
                 def add_line(side, t=t, q=q, cols=cols):
                     block = lanes_of(r.line_in.at[side, t, s], q)
-                    await_copy(block, r.sum_s.at[t, s, q], r.sum_r.at[side, t, s, q], on_z(1))
+                    await_bytes(block, r.sum_r.at[t, stream(s, zl, side), q])
                     r.total[t, s, :, cols] += r.line_in[side, t, s, :, cols].astype(F32)
 
                 @pl.when(jnp.logical_and(o >= zl, zl > 0))
@@ -713,8 +671,8 @@
                         lambda out=out, t=t, s=s, q=q, side=side: remote(
                             out,
                             lanes_of(r.line_in.at[side, t, s], q),
-                            r.sum_s.at[t, s, q],
-                            r.sum_r.at[side, t, s, q],
+                            r.sum_s.at[0],
+                            r.sum_r.at[t, stream(s, zl + 1 - 2 * side, side), q],
                             on_z(-1 if side else 1),
                         ),
                     )
@@ -723,13 +681,13 @@
                         lambda out=out, t=t, s=s, q=q, side=side: remote(
                             out,
                             lanes_of(r.ret.at[t], q),
-                            r.sum_s.at[t, s, q],
-                            r.ret_r.at[t, q],
+                            r.sum_s.at[0],
+                            r.ret_r.at[0],
                             ends[side],
                         ),
                     )
 
-    for p in (other, far_end, side_end, near):
+    for p in (other, far_end, third, fourth):
         collect(p)
         along(p)
 
@@ -738,8 +696,8 @@
         return remote(
             r.home_out.at[ring_x(d), cc, :, cols],
             r.home_in.at[x, :, cols],
-            r.home_s.at[side, d, cc],
-            r.home_r.at[side, d],
+            r.home_s.at[0],
+            r.home_r.at[1 if d else 0],
             at(z, y, ring_x(d), cc),
         )
 
@@ -752,10 +710,8 @@
             value = None
             for rel in range(2):
                 for t in range(2):
-                    if rel == 1 and side == 0:
-                        for q in range(2):
-                            block = lanes_of(r.ret.at[t], q)
-                            await_copy(block, r.sum_s.at[t, 0, q], r.ret_r.at[t, q], ends[0])
+                    if rel == 1 and side == 0 and t == 0:
+                        await_bytes(r.ret, r.ret_r.at[0])
                     rows = r.ret[t] if rel else r.line_out[t, near]
                     term = r.share[rel, t][:, 0:1] * dot(r.sel[rel, t, side], rows)
                     value = term if value is None else value + term
@@ -766,40 +722,61 @@
                 home_copy(side, d, cc).start()
         r.home[...] = r.mixed[x, c]
 
-    def home_wait(d):
-        for side in range(2):
-            cols = pl.ds(HALF * side, HALF)
-            block = r.home_in.at[ring_x(-d), :, cols]
-            await_copy(block, r.home_s.at[side, d, c], r.home_r.at[side, d], on_x(d))
-
     @pl.when(jnp.logical_not(source))
     def _():
-        home_wait(0)
+        await_bytes(r.home_in.at[0], r.home_r.at[0])
         r.home[...] = r.home_in[x].astype(F32)
 
     result = r.hidden[...] + r.home[...]
+    await_bytes(r.home_in.at[pl.ds(0, 3)], r.home_r.at[1])
     for d in (1, 3, 2):
-        home_wait(d)
         result = result + r.home_in[ring_x(-d)].astype(F32)
     r.out[...] = result.astype(BF16)
 
+    await_bytes(units(21), r.early_s.at[0])
+    await_bytes(r.slab_out.at[:, pl.ds(0, 3)], r.slab_s.at[0])
+    await_bytes(units(36), r.row_s.at[0])
+    for n, ref in enumerate((r.tokens, r.tables)):
+        await_bytes(ref.at[pl.ds(0, 3)], r.tok_s.at[n])
+    for d in range(1, NZ):
+
+        @pl.when(z + d == NZ - 1)
+        def _(d=d):
+            await_bytes(r.total_in.at[pl.ds(0, d)], r.total_s.at[0])
+
+    @pl.when(keeper)
+    def _():
+        await_bytes(r.gate, r.own_s.at[0])
+        await_bytes(r.gate.at[own_rows], r.own_s.at[1])
+
+    @pl.when(away)
+    def _():
+        for semaphore in (r.swap_s, r.pass_s):
+            await_bytes(r.gate, semaphore.at[0])
+            await_bytes(r.gate.at[own_rows], semaphore.at[1])
+
     @pl.when(source)
     def _():
-        for t in range(2):
-            for q in range(2):
-                cross_copy(t, q).wait_send()
-        for side in range(2):
-            for d, cc in home_targets:
-                home_copy(side, d, cc).wait_send()
-
-    for condition, make in guarded:
-
-        @pl.when(condition)
-        def _(make=make):
-            make().wait_send()
-
-    for copy in sends:
-        copy.wait_send()
+        await_bytes(units(3), r.cross_s.at[0])
+        await_bytes(units(9), r.sum_s.at[0])
+        await_bytes(units(7), r.home_s.at[0])
+
+    @pl.when(jnp.logical_not(source))
+    def _():
+        for n, ref in enumerate((r.tokens, r.tables)):
+            await_bytes(ref.at[0], r.tok_s.at[n + 2])
+        await_bytes(units(12), r.sum_s.at[0])
+
+    forwards = sum(
+        jnp.where(jnp.logical_and(origin(s) <= zl, zl < 3), 1, 0)
+        + jnp.where(jnp.logical_and(origin(s) >= zl, zl > 0), 1, 0)
+        for s in range(4)
+    )
+    for n in range(1, 9):
+
+        @pl.when(forwards == n)
+        def _(n=n):
+            await_bytes(units(3 * n), r.line_s.at[0])
 
 
 VMEM = pl.BlockSpec(memory_space=pltpu.VMEM)

time: 136 us -> 131 us (0.963); the launches traced: 134 us -> 131 us
  Pallas kernels: 132 us -> 130 us
    pallas_call x1, Pallas kernels: 132 us -> 130 us  [body(): pl.pallas_call(kernel, out_shape=jax.ShapeDtypeStruct(stream.shape, BF16)...]
where the time goes in v4:
time: 131 us
  Pallas kernels  130 us (99%)
  local copies, waits for them, and re-layouts  1.54 us (1%)
    pallas_call x1, Pallas kernels, body(): pl.pallas_call(kernel, out_shape=jax.ShapeDtypeStruct(stream.shape, BF16)...  130 us

profile of v4, /device:TPU:1, one launch (start us, length us, event | category | flops | bytes accessed | tf_op | source)
XLA Modules:
  0.0 131.2 jit_solution(10974886053455519129)
XLA Ops:
  0.0 129.6 %whole.1 = bf16[16,3072]{1,0:T(8,128)(2,1)} custom-call(bf16[16,3072]{1,0:T(8,128)(2,1)} %refs_0_.1, bf16[128,512]{1,0:T(8,128)(2,1)} %refs_1_.1, bf16[128,512]{1,0:T(8,128)(2,1)} %refs_2_.1, bf16[128,512]{1,0:T(8,128)(2,1)} %refs_3_.1, f32[1,4]{1,0:T(1,128)} %bitcast.13, bf16[96,512]{1,0:T(8,128)(2,1)} %bitcast.9, f32[1,3072]{1,0:T(1,128)} %bitcast.11, ...), custom_call_target="tpu_custom_call" | custom-call | tf_op jit(solution)/shard_map/whole/pallas_call | solution.py:800
  129.7 1.5 %copy.14 = bf16[16,3072]{1,0:T(8,128)(2,1)} copy(bf16[16,3072]{1,0:T(8,128)(2,1)} %whole.1) | data formatting | bytes 196608

commit v5 on v4

--- a/solution.py
+++ b/solution.py
@@ -18,10 +18,11 @@
 CHUNK = 48
 SHARD = 96
 HIDDEN = 288
-PIECES = 2
+PIECES = 4
 WIDTH = HALF // PIECES
 PIECE = 96
 PART = 48
+SHARD_ORDER = (0, 1, 7, 2, 6, 3, 5, 4)
 
 
 def bf(*shape):
@@ -37,10 +38,15 @@
 
 
 INPUTS = (
-    "stream", "query", "key", "value", "rates", "weight", "gain", "routes", "router",
-    "gate_hbm", "up_hbm", "down_hbm", "out",
+    "stream_hbm", "query", "key", "value", "rates_hbm", "weight", "gain_hbm", "routes_hbm",
+    "router_hbm", "gate_hbm", "up_hbm", "down_hbm", "out",
 )
 SCRATCH = dict(
+    stream=bf(16, DM),
+    rates=fl(1, 4),
+    gain=fl(1, DM),
+    routes=pltpu.VMEM((2, 16), jnp.int32),
+    router=bf(16, DM),
     intra=fl(4, 128, 128),
     key_in=bf(4, 128, 128),
     value_in=bf(4, 128, 128),
@@ -81,7 +87,7 @@
     home_out=bf(4, 2, 16, DM),
     home_in=bf(4, 16, DM),
     home=fl(16, DM),
-    early_s=dma(1), slab_s=dma(1), tok_s=dma(4), total_s=dma(1), own_s=dma(2),
+    load_r=dma(6), early_s=dma(1), slab_s=dma(1), tok_s=dma(4), total_s=dma(1), own_s=dma(2),
     swap_s=dma(2), pass_s=dma(2), cross_s=dma(1), line_s=dma(1), row_s=dma(1), sum_s=dma(1),
     home_s=dma(1),
     block_r=dma(4), total_r=dma(1), proj_r=dma(4), heads_r=dma(1), pair_r=dma(2), part_r=dma(2),
@@ -197,6 +203,23 @@
         hbm, ref = experts[m]
         return pltpu.make_async_copy(hbm, ref.at[own_rows], r.own_r.at[m // 2])
 
+    def head_columns(h):
+        return pl.ds(pl.multiple_of(h * 128, 128), 128)
+
+    blocks = ((r.key, r.key_in), (r.value, r.value_in), (r.query, r.query_in))
+    for whole, own in blocks:
+        pltpu.make_async_copy(whole.at[:, head_columns(y)], own.at[y], r.load_r.at[0]).start()
+    pltpu.make_async_copy(r.weight, r.proj.at[0], r.load_r.at[0]).start()
+    small = (
+        (r.rates_hbm, r.rates),
+        (r.stream_hbm, r.stream),
+        (r.gain_hbm, r.gain),
+        (r.routes_hbm, r.routes),
+        (r.router_hbm, r.router),
+    )
+    for n, (hbm, ref) in enumerate(small):
+        pltpu.make_async_copy(hbm, ref, r.load_r.at[n + 1]).start()
+
     @pl.when(keeper)
     def _():
         for m in range(3):
@@ -240,26 +263,6 @@
             await_bytes(r.gate, r.pass_r.at[0])
             await_bytes(r.gate.at[own_rows], r.pass_r.at[1])
 
-    rates = r.rates[...]
-    length = r.query.shape[0]
-    gap = (
-        lax.broadcasted_iota(jnp.int32, (length, length), 0)
-        - lax.broadcasted_iota(jnp.int32, (length, length), 1)
-    ).astype(F32)
-    position = lax.broadcasted_iota(jnp.int32, (length, 1), 0).astype(F32)
-    lane = lax.broadcasted_iota(jnp.int32, rates.shape, 1)
-    own_rate = jnp.sum(jnp.where(lane == y, rates, 0.0), axis=1, keepdims=True)
-
-    def power(n):
-        return jnp.exp(-own_rate * (128.0 * n))
-
-    def head_columns(h):
-        return pl.ds(pl.multiple_of(h * 128, 128), 128)
-
-    blocks = ((r.key, r.key_in), (r.value, r.value_in), (r.query, r.query_in))
-    for whole, own in blocks:
-        own[y] = whole[:, head_columns(y)]
-    r.proj[z] = r.weight[...]
     pl.semaphore_wait(barrier, NY - 1 + NZ - 1 + NX - 1 + NX + 3)
 
     for n, (whole, own) in enumerate(blocks):
@@ -274,15 +277,18 @@
                 )
             )
 
-    def z_parts(k):
-        if k < 4:
-            return r.proj.at[ring_z(1 - k)], r.proj.at[ring_z(k - 1)]
-        return r.proj.at[ring_z(-3)].at[pl.ds(0, 48)], r.proj.at[ring_z(3)].at[pl.ds(48, 48)]
+    def shard(distance):
+        return r.proj.at[SHARD_ORDER.index(distance % NZ)]
 
     def z_step(k):
-        a, b = z_parts(k)
-        launch(remote(a, a, r.early_s.at[0], r.proj_r.at[k - 1], on_z(1)))
-        launch(remote(b, b, r.early_s.at[0], r.proj_r.at[k - 1], on_z(-1)))
+        a, b, to_a, to_b = shard(1 - k), shard(k - 1), shard(-k), shard(k)
+        if k == 1:
+            a = b = r.weight
+        if k == 4:
+            a, to_a = a.at[pl.ds(0, 48)], to_a.at[pl.ds(0, 48)]
+            b, to_b = b.at[pl.ds(48, 48)], to_b.at[pl.ds(48, 48)]
+        launch(remote(a, to_a, r.early_s.at[0], r.proj_r.at[k - 1], on_z(1)))
+        launch(remote(b, to_b, r.early_s.at[0], r.proj_r.at[k - 1], on_z(-1)))
 
     def z_wait(k):
         await_bytes(r.proj.at[pl.ds(0, 2 if k < 4 else 1)], r.proj_r.at[k - 1])
@@ -296,6 +302,22 @@
                 experts[m][0], experts[m][1].at[own_rows], r.own_s.at[m // 2], r.own_r.at[m // 2], partner
             ),
         )
+
+    for n, (hbm, ref) in enumerate(small):
+        await_bytes(ref, r.load_r.at[n + 1])
+    await_bytes(units(2), r.load_r.at[0])
+    rates = r.rates[...]
+    length = r.query.shape[0]
+    gap = (
+        lax.broadcasted_iota(jnp.int32, (length, length), 0)
+        - lax.broadcasted_iota(jnp.int32, (length, length), 1)
+    ).astype(F32)
+    position = lax.broadcasted_iota(jnp.int32, (length, 1), 0).astype(F32)
+    lane = lax.broadcasted_iota(jnp.int32, rates.shape, 1)
+    own_rate = jnp.sum(jnp.where(lane == y, rates, 0.0), axis=1, keepdims=True)
+
+    def power(n):
+        return jnp.exp(-own_rate * (128.0 * n))
 
     fade = jnp.exp(-own_rate * (length - 1.0 - position))
     for d in (0, 1, 3, 2):
@@ -354,7 +376,6 @@
     swap(3)
     await_bytes(r.heads.at[pl.ds(0, 3)], r.heads_r.at[0])
     swap(1)
-    z_wait(4)
 
     def project(which, n):
         lhs = jnp.concatenate([r.heads[h, :, :, which].reshape(256, 128) for h in range(4)], axis=1)
@@ -362,9 +383,10 @@
         return nt_dot(lhs, rhs).reshape(4, 4, 16, 384)
 
     for n in range(2):
+        if n == 1:
+            z_wait(4)
         r.pair_out[n] = project(1 - c, n).astype(BF16)
         launch(remote(r.pair_out.at[n], r.pair_in.at[n], r.early_s.at[0], r.pair_r.at[n], partner))
-    for n in range(2):
         r.part[n] = project(c, n)
     for n in range(2):
         await_bytes(r.pair_in.at[n], r.pair_r.at[n])
@@ -404,9 +426,15 @@
         for d in (1, 3, 2):
             r.slab[n, ring_y(-d)] = r.slab_in[n, ring_y(-d)].astype(F32)
     swap(2)
+    def columns_of(yy):
+        places = [SHARD_ORDER.index(distance) for distance in range(NZ)]
+        ordered = [r.slab[p // 4, yy][:, SHARD * (p % 4) : SHARD * (p % 4 + 1)] for p in places]
+        return pltpu.roll(jnp.concatenate(ordered, axis=1), z * SHARD, 1)
+
+    quarters = [columns_of(yy) for yy in range(NY)]
     attended = jnp.concatenate(
         [
-            r.slab[zz // 4, yy][:, SHARD * (zz % 4) : SHARD * (zz % 4 + 1)]
+            quarters[yy][:, SHARD * zz : SHARD * (zz + 1)]
             for zz in range(NZ)
             for yy in range(NY)
         ],
@@ -507,9 +535,10 @@
                 else:
                     r.line[t, near] = chunk
 
+    swapped = edge * (core - c) * (core - c)
     order = [
-        near,
-        edge * (2 + near) + (1 - edge) * (1 - near),
+        near + 2 * swapped,
+        edge * (2 + near - 2 * swapped) + (1 - edge) * (1 - near),
         edge * (1 - near) + (1 - edge) * (2 + near),
         3 - near,
     ]
@@ -584,7 +613,6 @@
                 r.share[rel, t] = jnp.broadcast_to(share, (128, 128))
 
     other, side_end, far_end = 1 - near, 2 + near, 3 - near
-    swapped = edge * (core - c) * (core - c)
     third = side_end + swapped * (near - side_end)
     fourth = near + swapped * (side_end - near)
 
@@ -800,7 +828,7 @@
     return pl.pallas_call(
         kernel,
         out_shape=jax.ShapeDtypeStruct(stream.shape, BF16),
-        in_specs=[VMEM] * 9 + [ANY] * 3,
+        in_specs=[ANY] * 12,
         out_specs=VMEM,
         scratch_shapes=list(SCRATCH.values()),
         compiler_params=pltpu.CompilerParams(

time: 131 us -> 129 us (0.985)
  Pallas kernels: 130 us -> 127 us
    pallas_call x1, Pallas kernels: 130 us -> 127 us  [body(): pl.pallas_call(kernel, out_shape=jax.ShapeDtypeStruct(stream.shape, BF16)...]
where the time goes in v5:
time: 129 us; the launch traced here: 128 us
  Pallas kernels  127 us (98%)
  local copies, waits for them, and re-layouts  1.54 us (1%)
    pallas_call x1, Pallas kernels, body(): pl.pallas_call(kernel, out_shape=jax.ShapeDtypeStruct(stream.shape, BF16)...  127 us

profile of v5, /device:TPU:1, one launch (start us, length us, event | category | flops | bytes accessed | tf_op | source)
XLA Modules:
  0.0 128.4 jit_solution(18421176204288588947)
XLA Ops:
  0.0 126.9 %whole.1 = bf16[16,3072]{1,0:T(8,128)(2,1)} custom-call(bf16[16,3072]{1,0:T(8,128)(2,1)} %refs_0_.1, bf16[128,512]{1,0:T(8,128)(2,1)} %refs_1_.1, bf16[128,512]{1,0:T(8,128)(2,1)} %refs_2_.1, bf16[128,512]{1,0:T(8,128)(2,1)} %refs_3_.1, f32[1,4]{1,0:T(1,128)} %bitcast.13, bf16[96,512]{1,0:T(8,128)(2,1)} %bitcast.9, f32[1,3072]{1,0:T(1,128)} %bitcast.11, ...), custom_call_target="tpu_custom_call" | custom-call | tf_op jit(solution)/shard_map/whole/pallas_call | solution.py:828
  126.9 1.5 %copy.14 = bf16[16,3072]{1,0:T(8,128)(2,1)} copy(bf16[16,3072]{1,0:T(8,128)(2,1)} %whole.1) | data formatting | bytes 196608

commit v6 on v5

--- a/solution.py
+++ b/solution.py
@@ -79,6 +79,7 @@
     flat=bf(192, DM),
     partial=bf(4, 4, CHUNK, HALF),
     back=bf(3, 4, CHUNK, HALF),
+    extra=bf(CHUNK, HALF),
     total=fl(2, 4, CHUNK, HALF),
     line_out=bf(2, 4, CHUNK, HALF),
     line_in=bf(2, 2, 4, CHUNK, HALF),
@@ -92,7 +93,7 @@
     home_s=dma(1),
     block_r=dma(4), total_r=dma(1), proj_r=dma(4), heads_r=dma(1), pair_r=dma(2), part_r=dma(2),
     slab_r=dma(1), tok_r=dma(2), own_r=dma(2), swap_r=dma(4), pass_r=dma(2),
-    line_r=dma(2, 4, PIECES), got_r=dma(4), back_r=dma(4), sum_r=dma(2, 5, PIECES), ret_r=dma(1),
+    line_r=dma(2, 4, PIECES), got_r=dma(4), far_r=dma(4), back_r=dma(4), extra_r=dma(1), sum_r=dma(2, 5, PIECES), ret_r=dma(1),
     home_r=dma(2),
 )
 
@@ -543,6 +544,9 @@
         3 - near,
     ]
 
+    other, side_end, far_end = 1 - near, 2 + near, 3 - near
+    two_on = on_z(2 - 4 * near)
+
     def origin(s):
         outer = s // 2
         return (1 - outer) * (c + 2 * s) + outer * (5 * s - 11)
@@ -576,11 +580,16 @@
                             on_z(-1 if side else 1),
                         ),
                     )
-            for j, d, wanted in ((0, 2, role == t), (1, 1, role != t), (2, -1, role != t)):
+            straight = jnp.logical_and(role == t, s != far_end)
+            for j, d, wanted in ((0, 2, straight), (1, 1, role != t), (2, -1, role != t)):
                 launch_if(
                     wanted,
                     lambda block=block, s=s, j=j, d=d: remote(
-                        block, r.got.at[j, s], r.row_s.at[0], r.got_r.at[s], on_y(d)
+                        block,
+                        r.got.at[j, s],
+                        r.row_s.at[0],
+                        (r.got_r if j else r.far_r).at[s],
+                        on_y(d),
                     ),
                 )
 
@@ -590,6 +599,9 @@
     pass_on(3)
     spread(2)
     spread(3)
+    across = r.got.at[0, side_end]
+    await_bytes(across, r.far_r.at[side_end])
+    launch(remote(across, across, r.row_s.at[0], r.far_r.at[side_end], two_on))
 
     @pl.when(source)
     def _():
@@ -612,12 +624,13 @@
                 )
                 r.share[rel, t] = jnp.broadcast_to(share, (128, 128))
 
-    other, side_end, far_end = 1 - near, 2 + near, 3 - near
     third = side_end + swapped * (near - side_end)
     fourth = near + swapped * (side_end - near)
 
     def arrived(p):
-        await_bytes(r.got.at[:, p], r.got_r.at[p])
+        await_bytes(r.got.at[pl.ds(1, 2), p], r.got_r.at[p])
+        if p is not side_end:
+            await_bytes(r.got.at[0, p], r.far_r.at[p])
 
     def flatten(p, place):
         chunks = [r.line[role, p]] + [r.got[j, p] for j in range(3)]
@@ -638,8 +651,9 @@
                 rows = slice(SLOTS * (4 * n + j), SLOTS * (4 * n + j + 1))
                 r.partial[j, p] = jnp.concatenate([left[rows], right[rows]], axis=0).astype(BF16)
 
-    def give_back(p):
-        for j, d in ((0, 2), (1, -1), (2, 1)):
+    def give_back(p, ways=(0, 1, 2)):
+        for j in ways:
+            d = (2, -1, 1)[j]
             launch(
                 remote(
                     r.partial.at[j + 1, p], r.back.at[j, p], r.row_s.at[0], r.back_r.at[p], on_y(d)
@@ -658,12 +672,17 @@
     arrived(far_end)
     flatten(far_end, 0)
     compute((far_end, side_end))
-    for p in (far_end, third, fourth):
-        give_back(p)
+    launch(remote(r.partial.at[1, far_end], r.extra, r.row_s.at[0], r.extra_r.at[0], two_on))
+    give_back(far_end, (1, 2))
+    give_back(side_end, (1, 2))
 
     def collect(p):
-        await_bytes(r.back.at[:, p], r.back_r.at[p])
-        r.total[role, p] = r.partial[0, p].astype(F32) + r.back[0, p].astype(F32)
+        if p is far_end:
+            await_bytes(r.back.at[pl.ds(1, 2), p], r.back_r.at[p])
+            r.total[role, p] = r.partial[0, p].astype(F32)
+        else:
+            await_bytes(r.back.at[:, p], r.back_r.at[p])
+            r.total[role, p] = r.partial[0, p].astype(F32) + r.back[0, p].astype(F32)
         r.total[1 - role, p] = r.back[1, p].astype(F32) + r.back[2, p].astype(F32)
 
     ends = (at(lax.rem(4 * half + 4 + c, NZ), y, x, c), at(lax.rem(4 * half + 6 + c, NZ), y, x, c))
@@ -715,7 +734,23 @@
                         ),
                     )
 
-    for p in (other, far_end, third, fourth):
+    @pl.when(edge == 1)
+    def _():
+        collect(other)
+        along(other)
+
+    await_bytes(r.extra, r.extra_r.at[0])
+    joined = r.partial[1, side_end].astype(F32) + r.extra[...].astype(F32)
+    r.partial[1, side_end] = joined.astype(BF16)
+    give_back(side_end, (0,))
+    give_back(near)
+
+    @pl.when(edge == 0)
+    def _():
+        collect(other)
+        along(other)
+
+    for p in (far_end, third, fourth):
         collect(p)
         along(p)
 

time: 129 us -> 125 us (0.969)
  Pallas kernels: 127 us -> 123 us
    pallas_call x1, Pallas kernels: 127 us -> 123 us  [body(): pl.pallas_call(kernel, out_shape=jax.ShapeDtypeStruct(stream.shape, BF16)...]
where the time goes in v6:
time: 125 us
  Pallas kernels  123 us (98%)
  local copies, waits for them, and re-layouts  1.54 us (1%)
    pallas_call x1, Pallas kernels, body(): pl.pallas_call(kernel, out_shape=jax.ShapeDtypeStruct(stream.shape, BF16)...  123 us

profile of v6, /device:TPU:1, one launch (start us, length us, event | category | flops | bytes accessed | tf_op | source)
XLA Modules:
  0.0 124.7 jit_solution(2917495485113809105)
XLA Ops:
  0.0 123.2 %whole.1 = bf16[16,3072]{1,0:T(8,128)(2,1)} custom-call(bf16[16,3072]{1,0:T(8,128)(2,1)} %refs_0_.1, bf16[128,512]{1,0:T(8,128)(2,1)} %refs_1_.1, bf16[128,512]{1,0:T(8,128)(2,1)} %refs_2_.1, bf16[128,512]{1,0:T(8,128)(2,1)} %refs_3_.1, f32[1,4]{1,0:T(1,128)} %bitcast.13, bf16[96,512]{1,0:T(8,128)(2,1)} %bitcast.9, f32[1,3072]{1,0:T(1,128)} %bitcast.11, ...), custom_call_target="tpu_custom_call" | custom-call | tf_op jit(solution)/shard_map/whole/pallas_call | solution.py:863
  123.2 1.5 %copy.14 = bf16[16,3072]{1,0:T(8,128)(2,1)} copy(bf16[16,3072]{1,0:T(8,128)(2,1)} %whole.1) | data formatting | bytes 196608

commit v7 on v6

--- a/solution.py
+++ b/solution.py
@@ -18,7 +18,7 @@
 CHUNK = 48
 SHARD = 96
 HIDDEN = 288
-PIECES = 4
+PIECES = 3
 WIDTH = HALF // PIECES
 PIECE = 96
 PART = 48
@@ -317,6 +317,34 @@
     lane = lax.broadcasted_iota(jnp.int32, rates.shape, 1)
     own_rate = jnp.sum(jnp.where(lane == y, rates, 0.0), axis=1, keepdims=True)
 
+    square = lax.broadcasted_iota(jnp.int32, (16, 16), 0) == lax.broadcasted_iota(
+        jnp.int32, (16, 16), 1
+    )
+
+    def upright(row):
+        wide = jnp.where(square, jnp.broadcast_to(row, (16, 16)).astype(F32), 0.0)
+        return jnp.sum(wide, axis=1, keepdims=True)
+
+    table_lane = lax.broadcasted_iota(jnp.int32, (16, 128), 1)
+    r.tables[ep] = jnp.where(
+        table_lane == 0, upright(r.routes[0:1, :]), upright(r.routes[1:2, :])
+    ).astype(jnp.int32)
+
+    def gather(n, ref):
+        block = ref.at[ep]
+        for d in (2, 1, 3, 0):
+
+            def make(d=d):
+                device = at(z, y, ring_x(d), core)
+                return remote(block, block, r.tok_s.at[n if d else n + 2], r.tok_r.at[n], device)
+
+            if d:
+                launch(make())
+            else:
+                launch_if(jnp.logical_not(source), make)
+
+    gather(1, r.tables)
+
     def power(n):
         return jnp.exp(-own_rate * (128.0 * n))
 
@@ -375,6 +403,35 @@
     z_wait(3)
     z_step(4)
     swap(3)
+    low_lane = lax.broadcasted_iota(jnp.int32, (128, CHUNK), 1) < SLOTS
+
+    def expert_of(rel, t):
+        return x * 4 + t * 2 + (half if rel == 0 else 1 - half)
+
+    @pl.when(source)
+    def _():
+        await_bytes(r.tables.at[pl.ds(0, 7)], r.tok_r.at[1])
+        table = r.tables[...].reshape(128, 128)
+        first, second = table[:, 0:1], table[:, 1:2]
+        lanes = lax.broadcasted_iota(jnp.int32, (128, 128), 1)
+        earlier = (lanes < lax.broadcasted_iota(jnp.int32, (128, 128), 0)).astype(BF16)
+        pairs = [(1, 0), (1, 1), (0, 0), (0, 1)]
+        hits = []
+        for rel, t in pairs:
+            expert = expert_of(rel, t)
+            hits.append(jnp.where(jnp.logical_or(first == expert, second == expert), 1.0, 0.0))
+        wide = jnp.zeros((128, 128), F32)
+        for n, hit in enumerate(hits):
+            wide = jnp.where(lanes == n, hit, wide)
+        ranks = dot(earlier, wide.astype(BF16)).astype(jnp.int32)
+        slot = lax.broadcasted_iota(jnp.int32, (128, CHUNK), 1)
+        for n, (rel, t) in enumerate(pairs):
+            rank = ranks[:, n : n + 1]
+            low = jnp.where(slot == rank, hits[n], 0.0)
+            low = jnp.where(low_lane, low, 0.0).astype(BF16)
+            high = jnp.where(slot - SLOTS == rank, hits[n], 0.0).astype(BF16)
+            r.sel[rel, t, 0] = low
+            r.sel[rel, t, 1] = high
     await_bytes(r.heads.at[pl.ds(0, 3)], r.heads_r.at[0])
     swap(1)
 
@@ -389,7 +446,6 @@
         r.pair_out[n] = project(1 - c, n).astype(BF16)
         launch(remote(r.pair_out.at[n], r.pair_in.at[n], r.early_s.at[0], r.pair_r.at[n], partner))
         r.part[n] = project(c, n)
-    for n in range(2):
         await_bytes(r.pair_in.at[n], r.pair_r.at[n])
         both = r.part[n] + r.pair_in[n].astype(F32)
         r.part[n] = both
@@ -445,31 +501,7 @@
     r.hidden[...] = hidden
     mean = jnp.mean(hidden * hidden, axis=-1, keepdims=True)
     r.tokens[ep] = (hidden * lax.rsqrt(mean + EPSILON) * r.gain[...]).astype(BF16)
-    square = lax.broadcasted_iota(jnp.int32, (16, 16), 0) == lax.broadcasted_iota(
-        jnp.int32, (16, 16), 1
-    )
-
-    def upright(row):
-        wide = jnp.where(square, jnp.broadcast_to(row, (16, 16)).astype(F32), 0.0)
-        return jnp.sum(wide, axis=1, keepdims=True)
-
-    table_lane = lax.broadcasted_iota(jnp.int32, (16, 128), 1)
-    r.tables[ep] = jnp.where(
-        table_lane == 0, upright(r.routes[0:1, :]), upright(r.routes[1:2, :])
-    ).astype(jnp.int32)
-
-    for d in (2, 1, 3, 0):
-        for n, ref in enumerate((r.tokens, r.tables)):
-
-            def make(d=d, n=n, ref=ref):
-                block = ref.at[ep]
-                device = at(z, y, ring_x(d), core)
-                return remote(block, block, r.tok_s.at[n if d else n + 2], r.tok_r.at[n], device)
-
-            if d:
-                launch(make())
-            else:
-                launch_if(jnp.logical_not(source), make)
+    gather(0, r.tokens)
 
     pass_on(1)
 
@@ -489,43 +521,13 @@
             cross_to,
         )
 
-    low_lane = lax.broadcasted_iota(jnp.int32, (128, CHUNK), 1) < SLOTS
-
-    def expert_of(rel, t):
-        return x * 4 + t * 2 + (half if rel == 0 else 1 - half)
-
     @pl.when(source)
     def _():
-        for n, ref in enumerate((r.tokens, r.tables)):
-            await_bytes(ref.at[pl.ds(0, 7)], r.tok_r.at[n])
+        await_bytes(r.tokens.at[pl.ds(0, 7)], r.tok_r.at[0])
         rows = r.tokens[...].reshape(128, DM)
-        table = r.tables[...].reshape(128, 128)
-        first, second = table[:, 0:1], table[:, 1:2]
-        lanes = lax.broadcasted_iota(jnp.int32, (128, 128), 1)
-        earlier = (lanes < lax.broadcasted_iota(jnp.int32, (128, 128), 0)).astype(BF16)
-        pairs = [(1, 0), (1, 1), (0, 0), (0, 1)]
-        hits = []
-        for rel, t in pairs:
-            expert = expert_of(rel, t)
-            hits.append(jnp.where(jnp.logical_or(first == expert, second == expert), 1.0, 0.0))
-        wide = jnp.zeros((128, 128), F32)
-        for n, hit in enumerate(hits):
-            wide = jnp.where(lanes == n, hit, wide)
-        ranks = dot(earlier, wide.astype(BF16)).astype(jnp.int32)
-        slot = lax.broadcasted_iota(jnp.int32, (128, CHUNK), 1)
-        lows, highs = [], []
-        for n, (rel, t) in enumerate(pairs):
-            rank = ranks[:, n : n + 1]
-            low = jnp.where(slot == rank, hits[n], 0.0)
-            low = jnp.where(low_lane, low, 0.0).astype(BF16)
-            high = jnp.where(slot - SLOTS == rank, hits[n], 0.0).astype(BF16)
-            r.sel[rel, t, 0] = low
-            r.sel[rel, t, 1] = high
-            lows.append(low)
-            highs.append(high)
         for n in range(2):
-            low = jnp.concatenate(lows[2 * n : 2 * n + 2], axis=1)
-            high = jnp.concatenate(highs[2 * n : 2 * n + 2], axis=1)
+            low = jnp.concatenate([r.sel[1 - n, t, 0] for t in range(2)], axis=1)
+            high = jnp.concatenate([r.sel[1 - n, t, 1] for t in range(2)], axis=1)
             both = (tn_dot(low, rows[:, :HALF]) + tn_dot(high, rows[:, HALF:])).astype(BF16)
             for t in range(2):
                 chunk = both[CHUNK * t : CHUNK * (t + 1)]

time: 125 us -> 124 us (level)
  no operation moved by 1% of the time
where the time goes in v7:
time: 124 us
  Pallas kernels  123 us (99%)
  local copies, waits for them, and re-layouts  1.54 us (1%)
    pallas_call x1, Pallas kernels, body(): pl.pallas_call(kernel, out_shape=jax.ShapeDtypeStruct(stream.shape, BF16)...  123 us

profile of v7, /device:TPU:1, one launch (start us, length us, event | category | flops | bytes accessed | tf_op | source)
XLA Modules:
  0.0 124.4 jit_solution(13531089517838980264)
XLA Ops:
  0.0 122.8 %whole.1 = bf16[16,3072]{1,0:T(8,128)(2,1)} custom-call(bf16[16,3072]{1,0:T(8,128)(2,1)} %refs_0_.1, bf16[128,512]{1,0:T(8,128)(2,1)} %refs_1_.1, bf16[128,512]{1,0:T(8,128)(2,1)} %refs_2_.1, bf16[128,512]{1,0:T(8,128)(2,1)} %refs_3_.1, f32[1,4]{1,0:T(1,128)} %bitcast.13, bf16[96,512]{1,0:T(8,128)(2,1)} %bitcast.9, f32[1,3072]{1,0:T(1,128)} %bitcast.11, ...), custom_call_target="tpu_custom_call" | custom-call | tf_op jit(solution)/shard_map/whole/pallas_call | solution.py:865
  122.8 1.5 %copy.14 = bf16[16,3072]{1,0:T(8,128)(2,1)} copy(bf16[16,3072]{1,0:T(8,128)(2,1)} %whole.1) | data formatting | bytes 196608

commit v8 on v7

--- a/solution.py
+++ b/solution.py
@@ -72,7 +72,7 @@
     up=bf(2 * HIDDEN, DM),
     down=bf(2 * HIDDEN, DM),
     sel=bf(2, 2, 2, 128, CHUNK),
-    share=fl(2, 2, 128, 128),
+    weighted=bf(2, 128, 8 * CHUNK),
     cross=bf(2, CHUNK, HALF),
     line=bf(2, 4, CHUNK, HALF),
     got=bf(3, 4, CHUNK, HALF),
@@ -618,13 +618,21 @@
 
         lift_first, lift_second = lifted(first), lifted(second)
         both = lift_first + lift_second
+        shares = []
         for rel in range(2):
             for t in range(2):
                 chosen = expert_of(rel, t)
                 share = jnp.where(first == chosen, lift_first / both, 0.0) + jnp.where(
                     second == chosen, lift_second / both, 0.0
                 )
-                r.share[rel, t] = jnp.broadcast_to(share, (128, 128))
+                shares.append(share)
+        for side in range(2):
+            wide = jnp.concatenate(
+                [r.sel[n // 2, n % 2, side].astype(F32) * shares[n] for n in range(4)], axis=1
+            )
+            high = wide.astype(BF16)
+            low = (wide - high.astype(F32)).astype(BF16)
+            r.weighted[side] = jnp.concatenate([high, low], axis=1)
 
     third = side_end + swapped * (near - side_end)
     fourth = near + swapped * (side_end - near)
@@ -770,16 +778,11 @@
 
     @pl.when(source)
     def _():
+        await_bytes(r.ret, r.ret_r.at[0])
+        rows = jnp.concatenate([r.line_out[0, near], r.line_out[1, near], r.ret[0], r.ret[1]] * 2, axis=0)
         for side in range(2):
             cols = slice(HALF * side, HALF * (side + 1))
-            value = None
-            for rel in range(2):
-                for t in range(2):
-                    if rel == 1 and side == 0 and t == 0:
-                        await_bytes(r.ret, r.ret_r.at[0])
-                    rows = r.ret[t] if rel else r.line_out[t, near]
-                    term = r.share[rel, t][:, 0:1] * dot(r.sel[rel, t, side], rows)
-                    value = term if value is None else value + term
+            value = dot(r.weighted[side], rows)
             value = value.reshape(4, 2, 16, HALF)
             r.mixed[:, :, :, cols] = value
             r.home_out[:, :, :, cols] = value.astype(BF16)

time: 124 us -> 124 us (level)
  no operation moved by 1% of the time
where the time goes in v8:
time: 124 us
  Pallas kernels  123 us (99%)
  local copies, waits for them, and re-layouts  1.54 us (1%)
    pallas_call x1, Pallas kernels, body(): pl.pallas_call(kernel, out_shape=jax.ShapeDtypeStruct(stream.shape, BF16)...  123 us

profile of v8, /device:TPU:1, one launch (start us, length us, event | category | flops | bytes accessed | tf_op | source)
XLA Modules:
  0.0 124.4 jit_solution(410406495859976062)
XLA Ops:
  0.0 122.8 %whole.1 = bf16[16,3072]{1,0:T(8,128)(2,1)} custom-call(bf16[16,3072]{1,0:T(8,128)(2,1)} %refs_0_.1, bf16[128,512]{1,0:T(8,128)(2,1)} %refs_1_.1, bf16[128,512]{1,0:T(8,128)(2,1)} %refs_2_.1, bf16[128,512]{1,0:T(8,128)(2,1)} %refs_3_.1, f32[1,4]{1,0:T(1,128)} %bitcast.13, bf16[96,512]{1,0:T(8,128)(2,1)} %bitcast.9, f32[1,3072]{1,0:T(1,128)} %bitcast.11, ...), custom_call_target="tpu_custom_call" | custom-call | tf_op jit(solution)/shard_map/whole/pallas_call | solution.py:868
  122.8 1.5 %copy.14 = bf16[16,3072]{1,0:T(8,128)(2,1)} copy(bf16[16,3072]{1,0:T(8,128)(2,1)} %whole.1) | data formatting | bytes 196608
